TPU v7x, 256 devices: a whole 4x4x8 slice. The times are simulated.
256 devices in a mesh: dp: 4 (over y), expert: 64 (over x, z, core).
Axes of the slice: x: 4, y: 4, z: 8, core: 2. Of those that a mesh axis runs over, the one named last changes fastest.
Arguments:
- tokens: bfloat16 [8192, 2048], P(('dp', 'expert')), may hold values from -6 to 6
- expert_ids: int32 [8192, 8], P(('dp', 'expert')), may hold values from 0 to 63, all different within a row; in each aligned block of 32 rows (0 to 31, 32 to 63, ...) at most 6 rows name the same one
- route_gates: float32 [8192, 8], P(('dp', 'expert')), may hold values from 0.05 to 0.5
- gate_up: bfloat16 [64, 768, 2, 2048], P('expert', 'dp'), may hold values from -0.125 to 0.125
- down_weight: bfloat16 [64, 768, 2048], P('expert', 'dp'), may hold values from -0.21875 to 0.21875
- out_grad: bfloat16 [8192, 2048], P(('dp', 'expert')), may hold values from -6 to 6
Outputs:
- moe_out: bfloat16 [8192, 2048], P(('dp', 'expert'))
- gate_grad: float32 [8192, 8], P(('dp', 'expert'))
- token_grad: bfloat16 [8192, 2048], P(('dp', 'expert'))
- gate_up_grad: float32 [64, 768, 2, 2048], P('expert', 'dp')
- down_grad: float32 [64, 768, 2048], P('expert', 'dp')
Inputs may be any that keep to these rules, and one draw needn't show every extreme that they name: `expert_ids`: the rows of one device name no expert more than 6 times; in some device's rows some expert is named exactly 6 times. Each row names 8 different experts.
All inputs are finite; a program needn't handle non-finite values.
Results may differ from a plain program's by a relative error of at most 0.012.
Values may be sent and summed in bfloat16 or wider, within the bound.
No kernel may reach another device: no remote copies, remote signals or barrier semaphores. Data moves between devices by JAX's collectives and lax.ppermute only.
A program may use at most 128 MiB of HBM per device.

v0:
```python
import functools

import jax
import jax.numpy as jnp
from jax import lax
from jax.experimental import pallas as pl
from jax.experimental.pallas import tpu as pltpu
from jax.sharding import Mesh
from jax.sharding import PartitionSpec as P

F32 = jnp.float32
BF16 = jnp.bfloat16
LANES = 128
TILE = 512
LIMIT = 56 * 1024 * 1024
VMEM = pl.BlockSpec(memory_space=pltpu.VMEM)
SMEM = pl.BlockSpec(memory_space=pltpu.SMEM)
ANY = pl.BlockSpec(memory_space=pl.ANY)


def shift(value, axis, step):
    size = lax.axis_size(axis)
    return lax.ppermute(value, axis, [(i, (i + step) % size) for i in range(size)])


def dot(left, right, left_dim, right_dim):
    return lax.dot_general(
        left, right, (((left_dim,), (right_dim,)), ((), ())), preferred_element_type=F32
    )


def call(kernel, outs, in_specs, out_specs, scratch, flops, bytes_accessed, name):
    return pl.pallas_call(
        kernel,
        out_shape=[jax.ShapeDtypeStruct(s, d) for s, d in outs],
        in_specs=in_specs,
        out_specs=out_specs,
        scratch_shapes=scratch,
        compiler_params=pltpu.CompilerParams(vmem_limit_bytes=LIMIT),
        cost_estimate=pl.CostEstimate(
            flops=flops, bytes_accessed=bytes_accessed, transcendentals=0
        ),
        name=name,
    )


def split3(value):
    high = value.astype(BF16)
    rest = value - high.astype(F32)
    middle = rest.astype(BF16)
    low = (rest - middle.astype(F32)).astype(BF16)
    return high, middle, low


def pack_kernel(tokens, ids, gates, grads, packed):
    width = tokens.shape[1]
    top = ids.shape[1]
    row = lax.broadcasted_iota(jnp.int32, (top, LANES), 0)
    lane = lax.broadcasted_iota(jnp.int32, (top, LANES), 1)
    fields = (ids[...].astype(F32).astype(BF16),) + split3(gates[...])
    tail = jnp.zeros((tokens.shape[0], LANES), F32)
    for index, field in enumerate(fields):
        place = (lane == row + index * top).astype(F32).astype(BF16)
        tail = tail + dot(field, place, 1, 0)
    packed[:, :width] = tokens[...]
    packed[:, width : width + LANES] = tail.astype(BF16)
    packed[:, width + LANES :] = grads[...]


def select_kernel(top, dests, cap, z_index, *refs):
    blocks = refs[:8]
    send, pick_out, gate_out, place_out, held = refs[8:]
    rows = blocks[0].shape[0]
    width = send.shape[2]
    count = rows * len(blocks)
    for index, block in enumerate(blocks):
        held[index * rows : (index + 1) * rows, :] = block[...]
    info = held[:, width : width + LANES].astype(F32).T
    ids = info[:top]
    gates = info[top : 2 * top] + info[2 * top : 3 * top] + info[3 * top : 4 * top]
    order = lax.broadcasted_iota(jnp.int32, (top, count), 0).astype(F32)
    base = (z_index[0] * 2).astype(F32)
    marks, gate_rows, place_rows = [], [], []
    for dest in range(dests):
        expert = base + float((dest // 2) * 16 + dest % 2)
        chosen = ids == expert
        marks.append(jnp.sum(jnp.where(chosen, 1.0, 0.0), 0, keepdims=True))
        gate_rows.append(jnp.sum(jnp.where(chosen, gates, 0.0), 0, keepdims=True))
        place_rows.append(jnp.sum(jnp.where(chosen, order, 0.0), 0, keepdims=True))
    mark = jnp.concatenate(marks, 0)
    before = lax.broadcasted_iota(jnp.int32, (count, count), 0) < lax.broadcasted_iota(
        jnp.int32, (count, count), 1
    )
    rank = dot(mark.astype(BF16), before.astype(F32).astype(BF16), 1, 0)
    rank = jnp.where(mark > 0, rank, -1.0)
    slot = lax.broadcasted_iota(jnp.int32, (cap, count), 0).astype(F32)
    slot_gates = []
    for dest in range(dests):
        span = slice(dest * cap, (dest + 1) * cap)
        hit = rank[dest : dest + 1] == slot
        pick_out[span, :] = jnp.where(hit, 1.0, 0.0).astype(BF16)
        slot_gate = jnp.sum(jnp.where(hit, gate_rows[dest], 0.0), 1, keepdims=True)
        slot_place = jnp.sum(jnp.where(hit, place_rows[dest], 0.0), 1, keepdims=True)
        gate_out[span, :] = jnp.broadcast_to(slot_gate, (cap, LANES))
        place_out[span, :] = jnp.broadcast_to(slot_place, (cap, LANES))
        slot_gates.append(slot_gate)
    slot_gate = jnp.concatenate(slot_gates, 0)

    def columns(step, carry):
        first = pl.multiple_of(step * TILE, TILE)
        second = pl.multiple_of(step * TILE + width + LANES, LANES)
        pick = pick_out[...]
        tok = dot(pick, held[:, pl.ds(first, TILE)], 1, 0).astype(BF16)
        cot = (slot_gate * dot(pick, held[:, pl.ds(second, TILE)], 1, 0)).astype(BF16)
        send[:, :cap, pl.ds(first, TILE)] = tok.reshape(dests, cap, TILE)
        send[:, cap:, pl.ds(first, TILE)] = cot.reshape(dests, cap, TILE)
        return carry

    lax.fori_loop(0, width // TILE, columns, 0)


def expert_kernel(pieces_count, arrived, *refs):
    pieces = refs[:pieces_count]
    result = refs[pieces_count]
    grads = refs[pieces_count + 1 : 2 * pieces_count + 1]
    (x, c, w_gate, w_up, w_down, hid, gcot, ucot, hid_t, gcot_t, ucot_t, score, sems) = refs[
        2 * pieces_count + 1 :
    ]
    dests, double, width = arrived.shape
    cap = double // 2
    count = dests * cap
    half = pieces[0].shape[0] // 3
    units = half * pieces_count
    copies = [
        pltpu.make_async_copy(arrived.at[:, pl.ds(0, cap), :], x, sems.at[0]),
        pltpu.make_async_copy(arrived.at[:, pl.ds(cap, cap), :], c, sems.at[1]),
    ]
    for kind, weight in enumerate((w_gate, w_up, w_down)):
        for index, piece in enumerate(pieces):
            copies.append(
                pltpu.make_async_copy(
                    piece.at[pl.ds(kind * half, half), :],
                    weight.at[pl.ds(index * half, half), :],
                    sems.at[2 + kind * pieces_count + index],
                )
            )
    for copy in copies:
        copy.start()
    for copy in copies:
        copy.wait()
    score[...] = jnp.zeros_like(score)

    def unit_tile(step, carry):
        first = pl.multiple_of(step * 256, 256)
        span = pl.ds(first, 256)
        rows = x[...].reshape(count, width)
        gate_pre = dot(rows, w_gate[span, :], 1, 1)
        up_pre = dot(rows, w_up[span, :], 1, 1)
        hidden_cot = dot(c[...].reshape(count, width), w_down[span, :], 1, 1)
        sigma = jax.nn.sigmoid(gate_pre)
        silu = gate_pre * sigma
        hidden = (silu * up_pre).astype(BF16)
        gate_cot = hidden_cot * up_pre * sigma * (1.0 + gate_pre * (1.0 - sigma))
        up_cot = hidden_cot * silu
        hid[:, span] = hidden
        gcot[:, span] = gate_cot.astype(BF16)
        ucot[:, span] = up_cot.astype(BF16)
        hid_t[span, :] = hidden.astype(F32).T.astype(BF16)
        gcot_t[span, :] = gate_cot.T.astype(BF16)
        ucot_t[span, :] = up_cot.T.astype(BF16)
        both = hidden.astype(F32) * hidden_cot
        score[...] += both[:, :LANES] + both[:, LANES:]
        return carry

    lax.fori_loop(0, units // 256, unit_tile, 0)

    def columns(step, carry):
        first = pl.multiple_of(step * TILE, TILE)
        span = pl.ds(first, TILE)
        out = dot(hid[...], w_down[:, span], 1, 0)
        result[:, :cap, span] = out.astype(BF16).reshape(dests, cap, TILE)
        dx = dot(gcot[...], w_gate[:, span], 1, 0) + dot(ucot[...], w_up[:, span], 1, 0)
        result[:, cap:, span] = dx.astype(BF16).reshape(dests, cap, TILE)
        rows = x[:, :, span].reshape(count, TILE)
        cots = c[:, :, span].reshape(count, TILE)
        for kind, (left, right) in enumerate(((gcot_t, rows), (ucot_t, rows), (hid_t, cots))):
            grad = dot(left[...], right, 1, 0).astype(BF16)
            for index in range(pieces_count):
                grads[index][kind * half : (kind + 1) * half, span] = grad[
                    index * half : (index + 1) * half
                ]
        return carry

    lax.fori_loop(0, width // TILE, columns, 0)
    total = jnp.sum(score[...], 1, keepdims=True)
    lane = lax.broadcasted_iota(jnp.int32, (count, LANES), 1)
    high, middle, low = (part.astype(F32) for part in split3(total))
    tail = jnp.where(lane == 0, high, jnp.where(lane == 1, middle, jnp.where(lane == 2, low, 0.0)))
    result[:, cap:, width:] = tail.astype(BF16).reshape(dests, cap, LANES)
    result[:, :cap, width:] = jnp.zeros((dests, cap, LANES), BF16)


def combine_kernel(top, back, pick, slot_gate, slot_place, *blocks):
    dests, double, wide = back.shape
    width = wide - LANES
    cap = double // 2
    count = dests * cap
    rows = blocks[0].shape[0]
    gate = slot_gate[:, :1]

    def columns(step, carry):
        first = pl.multiple_of(step * TILE, TILE)
        second = pl.multiple_of(step * TILE + width + LANES, LANES)
        out = back[:, :cap, pl.ds(first, TILE)].reshape(count, TILE)
        dx = back[:, cap:, pl.ds(first, TILE)].reshape(count, TILE)
        weighted = (gate * out.astype(F32)).astype(BF16)
        moe = dot(pick[...], weighted, 0, 0).astype(BF16)
        grad = dot(pick[...], dx, 0, 0).astype(BF16)
        for index, block in enumerate(blocks):
            span = slice(index * rows, (index + 1) * rows)
            block[:, pl.ds(first, TILE)] = moe[span]
            block[:, pl.ds(second, TILE)] = grad[span]
        return carry

    lax.fori_loop(0, width // TILE, columns, 0)
    tail = back[:, cap:, width:].reshape(count, LANES).astype(F32)
    total = jnp.sum(tail, 1, keepdims=True) / jnp.where(gate > 0, gate, 1.0)
    lane = lax.broadcasted_iota(jnp.int32, (count, LANES), 1).astype(F32)
    spread = jnp.zeros((count, LANES), F32)
    for index, part in enumerate(split3(total)):
        spread = jnp.where(lane == slot_place[...] + float(index * top), part.astype(F32), spread)
    tail = dot(pick[...], spread.astype(BF16), 0, 0).astype(BF16)
    for index, block in enumerate(blocks):
        block[:, width : width + LANES] = tail[index * rows : (index + 1) * rows]


def ring_gather(block):
    size = lax.axis_size("z")
    right = [block]
    left = [block]
    for step in range(size // 2):
        right.append(shift(right[-1], "z", 1))
        if step < size - 1 - size // 2:
            left.append(shift(left[-1], "z", -1))
    return right + left[1:]


def add(left, right):
    return (left.astype(F32) + right.astype(F32)).astype(BF16)


def ring_reduce(blocks):
    far = lax.axis_size("z") // 2
    right = blocks[: far + 1]
    left = [blocks[0]] + blocks[far + 1 :]
    last = len(left) - 1
    carry_right = right[far]
    carry_left = left[last]
    for step in range(far):
        carry_right = shift(carry_right, "z", -1)
        if step < far - 1:
            carry_right = add(carry_right, right[far - 1 - step])
        if step < last:
            carry_left = shift(carry_left, "z", 1)
            if step < last - 1:
                carry_left = add(carry_left, left[last - 1 - step])
    return blocks[0].astype(F32) + carry_right.astype(F32) + carry_left.astype(F32)


def body(tokens, expert_ids, route_gates, gate_up, down_weight, out_grad):
    tok_count, width = tokens.shape
    top = expert_ids.shape[1]
    z_size = lax.axis_size("z")
    dests = lax.axis_size("x") * 2
    cap = 6 * z_size
    count = dests * cap
    held = tok_count * z_size
    units = gate_up.shape[1]
    half = units // 2
    wide = 2 * width + LANES

    w_gate, w_up, w_down = gate_up[0, :, 0, :], gate_up[0, :, 1, :], down_weight[0]
    own = [
        jnp.concatenate([w_gate[s], w_up[s], w_down[s]], 0)
        for s in (slice(0, half), slice(half, units))
    ]
    before_0 = shift(own[0], "dp", 1)
    after_1 = shift(own[1], "dp", -1)
    before_1 = shift(own[1], "dp", 1)
    after_0 = shift(own[0], "dp", -1)
    far_0 = shift(before_0, "dp", 1)
    far_1 = shift(after_1, "dp", -1)
    pieces = [own[0], own[1], before_0, before_1, after_0, after_1, far_0, far_1]

    (packed,) = call(
        pack_kernel, [((tok_count, wide), BF16)], [VMEM] * 4, [VMEM], [], 10**6, 6 * 10**5, "pack"
    )(tokens, expert_ids, route_gates, out_grad)
    blocks = ring_gather(packed)
    z_index = lax.axis_index("z").astype(jnp.int32).reshape(1)
    send, pick, slot_gate, slot_place = call(
        functools.partial(select_kernel, top, dests, cap),
        [
            ((dests, 2 * cap, width), BF16),
            ((count, held), BF16),
            ((count, LANES), F32),
            ((count, LANES), F32),
        ],
        [SMEM] + [VMEM] * len(blocks),
        [VMEM] * 4,
        [pltpu.VMEM((held, wide), BF16)],
        4 * count * held * width,
        6 * 10**6,
        "select",
    )(z_index, *blocks)
    arrived = lax.all_to_all(send, ("x", "c"), 0, 0, tiled=True)

    n = len(pieces)
    full = n * half
    result, *grads = call(
        functools.partial(expert_kernel, n),
        [((dests, 2 * cap, width + LANES), BF16)] + [((3 * half, width), BF16)] * n,
        [ANY] * (1 + n),
        [VMEM] * (1 + n),
        [pltpu.VMEM((dests, cap, width), BF16)] * 2
        + [pltpu.VMEM((full, width), BF16)] * 3
        + [pltpu.VMEM((count, full), BF16)] * 3
        + [pltpu.VMEM((full, count), BF16)] * 3
        + [pltpu.VMEM((count, LANES), F32), pltpu.SemaphoreType.DMA((2 + 3 * n,))],
        18 * count * full * width,
        25 * 10**6,
        "expert",
    )(arrived, *pieces)

    own_0, own_1, before_g0, before_g1, after_g0, after_g1, far_g0, far_g1 = grads
    relay_0 = shift(far_g0, "dp", 1)
    relay_1 = shift(far_g1, "dp", -1)
    got_before_1 = shift(after_g1, "dp", 1)
    got_after_0 = shift(before_g0, "dp", -1)
    got_before_0 = shift(add(after_g0, relay_0), "dp", 1)
    got_after_1 = shift(add(before_g1, relay_1), "dp", -1)
    total_0 = own_0.astype(F32) + got_before_0.astype(F32) + got_after_0.astype(F32)
    total_1 = own_1.astype(F32) + got_before_1.astype(F32) + got_after_1.astype(F32)

    def both(index):
        s = slice(index * half, (index + 1) * half)
        return jnp.concatenate([total_0[s], total_1[s]], 0)

    gate_up_grad = jnp.stack([both(0), both(1)], 1)[None]
    down_grad = both(2)[None]

    back = lax.all_to_all(result, ("x", "c"), 0, 0, tiled=True)
    parts = call(
        functools.partial(combine_kernel, top),
        [((tok_count, wide), BF16)] * z_size,
        [VMEM] * 4,
        [VMEM] * z_size,
        [],
        4 * count * held * width,
        6 * 10**6,
        "combine",
    )(back, pick, slot_gate, slot_place)
    summed = ring_reduce(list(parts))
    moe_out = summed[:, :width].astype(BF16)
    tail = summed[:, width : width + LANES]
    token_grad = summed[:, width + LANES :].astype(BF16)
    gate_grad = tail[:, :top] + tail[:, top : 2 * top] + tail[:, 2 * top : 3 * top]
    return moe_out, gate_grad, token_grad, gate_up_grad, down_grad


def solution(mesh):
    wide = Mesh(mesh.devices.reshape(4, 4, 8, 2), ("dp", "x", "z", "c"))
    expert = ("x", "z", "c")
    every = ("dp",) + expert
    in_specs = (
        P(every, None),
        P(every, None),
        P(every, None),
        P(expert, "dp", None, None),
        P(expert, "dp", None),
        P(every, None),
    )
    out_specs = (
        P(every, None),
        P(every, None),
        P(every, None),
        P(expert, "dp", None, None),
        P(expert, "dp", None),
    )
    return jax.shard_map(body, mesh=wide, in_specs=in_specs, out_specs=out_specs, check_vma=False)
```

profile of v0, /device:TPU:1, one launch (start us, length us, event | category | flops | bytes accessed | tf_op | source)
XLA Modules:
  0.0 283.1 jit_solution(13977376199827122864)
XLA Ops:
  7.7 3.9 %collective-permute-start.4 = (bf16[32,4224]{1,0:T(8,128)(2,1)}, bf16[32,4224]{1,0:T(8,128)(2,1)S(1)}, u32[]{:S(2)}, u32[]{:S(2)}) collective-permute-start(bf16[32,4224]{1,0:T(8,128)(2,1)} %pack.1.refs_0_), channel_id=1, source_target_pairs={{0,14},{2,0},{4,2},{6,4},{8,6},{10,8},{12,10},{14,12},{1,15},{3,1}... | collective-permute-start | bytes 811016 | tf_op jit(solution)/shard_map/ppermute | solution.py:23
  11.6 6.4 %collective-permute-done.refs_1_ = bf16[32,4224]{1,0:T(8,128)(2,1)S(1)} collective-permute-done((bf16[32,4224]{1,0:T(8,128)(2,1)}, bf16[32,4224]{1,0:T(8,128)(2,1)S(1)}, u32[]{:S(2)}, u32[]{:S(2)}) %collective-permute-start) | collective-permute-done | bytes 270368 | tf_op jit(solution)/shard_map/ppermute | solution.py:23
  18.0 5.4 %fusion.3 = (bf16[1,96,1,2048]{3,2,1,0:T(2,128)(2,1)}, bf16[1,96,1,2048]{3,2,1,0:T(2,128)(2,1)S(1)}, bf16[1,96,1,2048]{3,2,1,0:T(2,128)(2,1)S(1)}, bf16[1,96,1,2048]{3,2,1,0:T(2,128)(2,1)}) fusion(bf16[1,192,2,2048]{3,2,1,0:T(2,128)(2,1)} %param.9), kind=kLoop, calls=%fused_computation.27 | loop fusion | bytes 3145728 | tf_op jit(solution)/shard_map/slice | solution.py:284
  23.5 2.7 collective-permute-start.5
  26.7 3.8 %collective-permute-done.5.refs_6_ = bf16[32,4224]{1,0:T(8,128)(2,1)S(1)} collective-permute-done((bf16[32,4224]{1,0:T(8,128)(2,1)S(1)}, bf16[32,4224]{1,0:T(8,128)(2,1)S(1)}, u32[]{:S(2)}, u32[]{:S(2)}) %collective-permute-start.5) | collective-permute-done | bytes 270368 | tf_op jit(solution)/shard_map/ppermute | solution.py:23
  30.5 3.4 %collective-permute-start.6 = (bf16[32,4224]{1,0:T(8,128)(2,1)S(1)}, bf16[32,4224]{1,0:T(8,128)(2,1)S(1)}, u32[]{:S(2)}, u32[]{:S(2)}) collective-permute-start(bf16[32,4224]{1,0:T(8,128)(2,1)S(1)} %collective-permute-done.5.refs_6_), channel_id=1, source_target_pairs={{0,14},{2,0},{4,2},{6,4},{8,6},{10,8},{12,10},{14,12},{1,15},{3,1}... | collective-permute-start | bytes 811016 | tf_op jit(solution)/shard_map/ppermute | solution.py:23
  37.3 3.1 %collective-permute-done.3.refs_4_ = bf16[32,4224]{1,0:T(8,128)(2,1)S(1)} collective-permute-done((bf16[32,4224]{1,0:T(8,128)(2,1)S(1)}, bf16[32,4224]{1,0:T(8,128)(2,1)S(1)}, u32[]{:S(2)}, u32[]{:S(2)}) %collective-permute-start.3) | collective-permute-done | bytes 270368 | tf_op jit(solution)/shard_map/ppermute | solution.py:23
  41.1 5.2 %select.1 = (bf16[8,96,2048]{2,1,0:T(8,128)(2,1)}, bf16[384,256]{1,0:T(8,128)(2,1)}, f32[384,128]{1,0:T(8,128)}, f32[384,128]{1,0:T(8,128)}) custom-call(s32[1]{0:T(128)} %bitcast.z_index, bf16[32,4224]{1,0:T(8,128)(2,1)} %pack.1.refs_0_, bf16[32,4224]{1,0:T(8,128)(2,1)} %copy-done.22, bf16[32,4224]{1,0:T(8,128)(2,1)} %copy-done.24, ...), custom_call_target="tpu_custom_call" | custom-call | flops 805306368 | bytes 6000000 | tf_op jit(solution)/shard_map/select/pallas_call | solution.py:300
  46.4 8.2 %all-to-all-start = ((bf16[8,96,2048]{2,1,0:T(8,128)(2,1)}), bf16[8,96,2048]{2,1,0:T(8,128)(2,1)S(1)}, u32[]{:S(2)}, u32[]{:S(2)}) async-start(bf16[8,96,2048]{2,1,0:T(8,128)(2,1)} %get-tuple-element.26), calls=%async_computation | async-start | bytes 6291456 | tf_op jit(solution)/shard_map/all_to_all | solution.py:315
  56.5 2.8 collective-permute-start.10
  61.5 23.2 %collective-permute-done.10.refs_5_ = bf16[288,2048]{1,0:T(8,128)(2,1)S(1)} collective-permute-done((bf16[288,2048]{1,0:T(8,128)(2,1)S(1)}, bf16[288,2048]{1,0:T(8,128)(2,1)S(1)}, u32[]{:S(2)}, u32[]{:S(2)}) %collective-permute-start.10) | collective-permute-done | bytes 1179680 | tf_op jit(solution)/shard_map/ppermute | solution.py:23
  84.7 3.4 %collective-permute-start.12 = (bf16[288,2048]{1,0:T(8,128)(2,1)S(1)}, bf16[288,2048]{1,0:T(8,128)(2,1)}, u32[]{:S(2)}, u32[]{:S(2)}) collective-permute-start(bf16[288,2048]{1,0:T(8,128)(2,1)S(1)} %collective-permute-done.10.refs_5_), channel_id=1, source_target_pairs={{0,192},{64,0},{128,64},{192,128},{1,193},{65,1},{129,65},{193,129... | collective-permute-start | bytes 3538952 | tf_op jit(solution)/shard_map/ppermute | solution.py:23
  88.1 22.0 %collective-permute-done.9.refs_4_ = bf16[288,2048]{1,0:T(8,128)(2,1)S(1)} collective-permute-done((bf16[288,2048]{1,0:T(8,128)(2,1)}, bf16[288,2048]{1,0:T(8,128)(2,1)S(1)}, u32[]{:S(2)}, u32[]{:S(2)}) %collective-permute-start.9) | collective-permute-done | bytes 1179680 | tf_op jit(solution)/shard_map/ppermute | solution.py:23
  110.1 4.2 %collective-permute-done.11.refs_6_ = bf16[288,2048]{1,0:T(8,128)(2,1)S(1)} collective-permute-done((bf16[288,2048]{1,0:T(8,128)(2,1)}, bf16[288,2048]{1,0:T(8,128)(2,1)S(1)}, u32[]{:S(2)}, u32[]{:S(2)}) %collective-permute-start.11) | collective-permute-done | bytes 1179680 | tf_op jit(solution)/shard_map/ppermute | solution.py:23
  115.4 19.9 %collective-permute-done.12.refs_7_ = bf16[288,2048]{1,0:T(8,128)(2,1)} collective-permute-done((bf16[288,2048]{1,0:T(8,128)(2,1)S(1)}, bf16[288,2048]{1,0:T(8,128)(2,1)}, u32[]{:S(2)}, u32[]{:S(2)}) %collective-permute-start.12) | collective-permute-done | bytes 1179680 | tf_op jit(solution)/shard_map/ppermute | solution.py:23
  136.9 23.4 %expert.1 = (bf16[8,96,2176]{2,1,0:T(8,128)(2,1)}, bf16[288,2048]{1,0:T(8,128)(2,1)}, bf16[288,2048]{1,0:T(8,128)(2,1)}, bf16[288,2048]{1,0:T(8,128)(2,1)}, bf16...) custom-call(bf16[8,96,2048]{2,1,0:T(8,128)(2,1)} %copy-done.1, ...), custom_call_target="tpu_custom_call" | custom-call | flops 10871635968 | bytes 25000000 | tf_op jit(solution)/shard_map/expert/pallas_call | solution.py:319
  161.3 2.7 collective-permute-start.24
  165.4 24.3 %collective-permute-done.20 = bf16[288,2048]{1,0:T(8,128)(2,1)S(1)} collective-permute-done((bf16[288,2048]{1,0:T(8,128)(2,1)}, bf16[288,2048]{1,0:T(8,128)(2,1)S(1)}, u32[]{:S(2)}, u32[]{:S(2)}) %collective-permute-start.20) | collective-permute-done | bytes 1179680 | tf_op jit(solution)/shard_map/ppermute | solution.py:23
  192.5 5.4 %all-to-all-start.1 = ((bf16[8,96,2176]{2,1,0:T(8,128)(2,1)}), bf16[8,96,2176]{2,1,0:T(8,128)(2,1)S(1)}, u32[]{:S(2)}, u32[]{:S(2)}) async-start(bf16[8,96,2176]{2,1,0:T(8,128)(2,1)} %get-tuple-element.27), calls=%async_computation.1 | async-start | bytes 6684672 | tf_op jit(solution)/shard_map/all_to_all | solution.py:351
  203.1 11.0 %collective-permute-done.22 = bf16[288,2048]{1,0:T(8,128)(2,1)} collective-permute-done((bf16[288,2048]{1,0:T(8,128)(2,1)}, bf16[288,2048]{1,0:T(8,128)(2,1)}, u32[]{:S(2)}, u32[]{:S(2)}) %collective-permute-start.22) | collective-permute-done | bytes 1179680 | tf_op jit(solution)/shard_map/ppermute | solution.py:23
  214.2 5.9 %collective-permute-done.21 = bf16[288,2048]{1,0:T(8,128)(2,1)} collective-permute-done((bf16[288,2048]{1,0:T(8,128)(2,1)}, bf16[288,2048]{1,0:T(8,128)(2,1)}, u32[]{:S(2)}, u32[]{:S(2)}) %collective-permute-start.21) | collective-permute-done | bytes 1179680 | tf_op jit(solution)/shard_map/ppermute | solution.py:23
  223.9 21.4 %collective-permute-done.23 = bf16[288,2048]{1,0:T(8,128)(2,1)S(1)} collective-permute-done((bf16[288,2048]{1,0:T(8,128)(2,1)}, bf16[288,2048]{1,0:T(8,128)(2,1)S(1)}, u32[]{:S(2)}, u32[]{:S(2)}) %collective-permute-start.23) | collective-permute-done | bytes 1179680 | tf_op jit(solution)/shard_map/ppermute | solution.py:23
  249.1 6.1 %combine.1 = (bf16[32,4224]{1,0:T(8,128)(2,1)}, bf16[32,4224]{1,0:T(8,128)(2,1)}, bf16[32,4224]{1,0:T(8,128)(2,1)}, bf16[32,4224]{1,0:T(8,128)(2,1)}, bf16[32,42...) custom-call(bf16[8,96,2176]{2,1,0:T(8,128)(2,1)} %copy-done, ...), custom_call_target="tpu_custom_call" | custom-call | flops 805306368 | bytes 6000000 | tf_op jit(solution)/shard_map/combine/pallas_call | solution.py:352
  276.2 4.1 %copy.18 = f32[1,192,2,2048]{3,2,1,0:T(2,128)} copy(f32[1,192,2,2048]{3,1,2,0:T(8,128)S(1)} %maximum_bitcast_fusion) | data formatting | bytes 6291456
  (124 shorter events, 60.0 us)
Async XLA Ops:
  5.2 12.8 %collective-permute-start = (bf16[32,4224]{1,0:T(8,128)(2,1)}, bf16[32,4224]{1,0:T(8,128)(2,1)S(1)}, u32[]{:S(2)}, u32[]{:S(2)}) collective-permute-start(bf16[32,4224]{1,0:T(8,128)(2,1)} %pack.1.refs_0_), channel_id=1, source_target_pairs={{0,2},{2,4},{4,6},{6,8},{8,10},{10,12},{12,14},{14,0},{1,3},{3,5},... | collective-permute-start | bytes 811016 | tf_op jit(solution)/shard_map/ppermute | solution.py:23
  7.7 15.8 %collective-permute-start.4 = (bf16[32,4224]{1,0:T(8,128)(2,1)}, bf16[32,4224]{1,0:T(8,128)(2,1)S(1)}, u32[]{:S(2)}, u32[]{:S(2)}) collective-permute-start(bf16[32,4224]{1,0:T(8,128)(2,1)} %pack.1.refs_0_), channel_id=1, source_target_pairs={{0,14},{2,0},{4,2},{6,4},{8,6},{10,8},{12,10},{14,12},{1,15},{3,1}... | collective-permute-start | bytes 811016 | tf_op jit(solution)/shard_map/ppermute | solution.py:23
  18.0 8.2 %collective-permute-start.1 = (bf16[32,4224]{1,0:T(8,128)(2,1)S(1)}, bf16[32,4224]{1,0:T(8,128)(2,1)S(1)}, u32[]{:S(2)}, u32[]{:S(2)}) collective-permute-start(bf16[32,4224]{1,0:T(8,128)(2,1)S(1)} %collective-permute-done.refs_1_), channel_id=1, source_target_pairs={{0,2},{2,4},{4,6},{6,8},{8,10},{10,12},{12,14},{14,0},{1,3},{3,5},... | collective-permute-start | bytes 811016 | tf_op jit(solution)/shard_map/ppermute | solution.py:23
  23.5 7.0 %collective-permute-start.5 = (bf16[32,4224]{1,0:T(8,128)(2,1)S(1)}, bf16[32,4224]{1,0:T(8,128)(2,1)S(1)}, u32[]{:S(2)}, u32[]{:S(2)}) collective-permute-start(bf16[32,4224]{1,0:T(8,128)(2,1)S(1)} %collective-permute-done.4.refs_5_), channel_id=1, source_target_pairs={{0,14},{2,0},{4,2},{6,4},{8,6},{10,8},{12,10},{14,12},{1,15},{3,1}... | collective-permute-start | bytes 811016 | tf_op jit(solution)/shard_map/ppermute | solution.py:23
  26.2 7.7 %collective-permute-start.2 = (bf16[32,4224]{1,0:T(8,128)(2,1)S(1)}, bf16[32,4224]{1,0:T(8,128)(2,1)S(1)}, u32[]{:S(2)}, u32[]{:S(2)}) collective-permute-start(bf16[32,4224]{1,0:T(8,128)(2,1)S(1)} %collective-permute-done.1.refs_2_), channel_id=1, source_target_pairs={{0,2},{2,4},{4,6},{6,8},{8,10},{10,12},{12,14},{14,0},{1,3},{3,5},... | collective-permute-start | bytes 811016 | tf_op jit(solution)/shard_map/ppermute | solution.py:23
  30.5 6.8 %collective-permute-start.6 = (bf16[32,4224]{1,0:T(8,128)(2,1)S(1)}, bf16[32,4224]{1,0:T(8,128)(2,1)S(1)}, u32[]{:S(2)}, u32[]{:S(2)}) collective-permute-start(bf16[32,4224]{1,0:T(8,128)(2,1)S(1)} %collective-permute-done.5.refs_6_), channel_id=1, source_target_pairs={{0,14},{2,0},{4,2},{6,4},{8,6},{10,8},{12,10},{14,12},{1,15},{3,1}... | collective-permute-start | bytes 811016 | tf_op jit(solution)/shard_map/ppermute | solution.py:23
  33.9 6.5 %collective-permute-start.3 = (bf16[32,4224]{1,0:T(8,128)(2,1)S(1)}, bf16[32,4224]{1,0:T(8,128)(2,1)S(1)}, u32[]{:S(2)}, u32[]{:S(2)}) collective-permute-start(bf16[32,4224]{1,0:T(8,128)(2,1)S(1)} %collective-permute-done.2.refs_3_), channel_id=1, source_target_pairs={{0,2},{2,4},{4,6},{6,8},{8,10},{10,12},{12,14},{14,0},{1,3},{3,5},... | collective-permute-start | bytes 811016 | tf_op jit(solution)/shard_map/ppermute | solution.py:23
  35.1 26.4 %collective-permute-start.7 = (bf16[288,2048]{1,0:T(8,128)(2,1)}, bf16[288,2048]{1,0:T(8,128)(2,1)}, u32[]{:S(2)}, u32[]{:S(2)}) collective-permute-start(bf16[288,2048]{1,0:T(8,128)(2,1)} %pad_maximum_fusion.refs_0_), channel_id=1, source_target_pairs={{0,64},{64,128},{128,192},{192,0},{1,65},{65,129},{129,193},{193,1... | collective-permute-start | bytes 3538952 | tf_op jit(solution)/shard_map/ppermute | solution.py:23
  46.4 88.9 %all-to-all-start = ((bf16[8,96,2048]{2,1,0:T(8,128)(2,1)}), bf16[8,96,2048]{2,1,0:T(8,128)(2,1)S(1)}, u32[]{:S(2)}, u32[]{:S(2)}) async-start(bf16[8,96,2048]{2,1,0:T(8,128)(2,1)} %get-tuple-element.26), calls=%async_computation | async-start | bytes 6291456 | tf_op jit(solution)/shard_map/all_to_all | solution.py:315
  56.5 28.2 %collective-permute-start.10 = (bf16[288,2048]{1,0:T(8,128)(2,1)S(1)}, bf16[288,2048]{1,0:T(8,128)(2,1)S(1)}, u32[]{:S(2)}, u32[]{:S(2)}) collective-permute-start(bf16[288,2048]{1,0:T(8,128)(2,1)S(1)} %pad_maximum_fusion.1.refs_1_), channel_id=1, source_target_pairs={{0,192},{64,0},{128,64},{192,128},{1,193},{65,1},{129,65},{193,129... | collective-permute-start | bytes 3538952 | tf_op jit(solution)/shard_map/ppermute | solution.py:23
  59.3 50.8 %collective-permute-start.9 = (bf16[288,2048]{1,0:T(8,128)(2,1)}, bf16[288,2048]{1,0:T(8,128)(2,1)S(1)}, u32[]{:S(2)}, u32[]{:S(2)}) collective-permute-start(bf16[288,2048]{1,0:T(8,128)(2,1)} %pad_maximum_fusion.refs_0_), channel_id=1, source_target_pairs={{0,192},{64,0},{128,64},{192,128},{1,193},{65,1},{129,65},{193,129... | collective-permute-start | bytes 3538952 | tf_op jit(solution)/shard_map/ppermute | solution.py:23
  59.8 50.3 %collective-permute-start.8 = (bf16[288,2048]{1,0:T(8,128)(2,1)S(1)}, bf16[288,2048]{1,0:T(8,128)(2,1)S(1)}, u32[]{:S(2)}, u32[]{:S(2)}) collective-permute-start(bf16[288,2048]{1,0:T(8,128)(2,1)S(1)} %pad_maximum_fusion.1.refs_1_), channel_id=1, source_target_pairs={{0,64},{64,128},{128,192},{192,0},{1,65},{65,129},{129,193},{193,1... | collective-permute-start | bytes 3538952 | tf_op jit(solution)/shard_map/ppermute | solution.py:23
  61.5 52.8 %collective-permute-start.11 = (bf16[288,2048]{1,0:T(8,128)(2,1)}, bf16[288,2048]{1,0:T(8,128)(2,1)S(1)}, u32[]{:S(2)}, u32[]{:S(2)}) collective-permute-start(bf16[288,2048]{1,0:T(8,128)(2,1)} %collective-permute-done.7.refs_2_), channel_id=1, source_target_pairs={{0,64},{64,128},{128,192},{192,0},{1,65},{65,129},{129,193},{193,1... | collective-permute-start | bytes 3538952 | tf_op jit(solution)/shard_map/ppermute | solution.py:23
  84.7 50.6 %collective-permute-start.12 = (bf16[288,2048]{1,0:T(8,128)(2,1)S(1)}, bf16[288,2048]{1,0:T(8,128)(2,1)}, u32[]{:S(2)}, u32[]{:S(2)}) collective-permute-start(bf16[288,2048]{1,0:T(8,128)(2,1)S(1)} %collective-permute-done.10.refs_5_), channel_id=1, source_target_pairs={{0,192},{64,0},{128,64},{192,128},{1,193},{65,1},{129,65},{193,129... | collective-permute-start | bytes 3538952 | tf_op jit(solution)/shard_map/ppermute | solution.py:23
  160.4 29.4 %collective-permute-start.20 = (bf16[288,2048]{1,0:T(8,128)(2,1)}, bf16[288,2048]{1,0:T(8,128)(2,1)S(1)}, u32[]{:S(2)}, u32[]{:S(2)}) collective-permute-start(bf16[288,2048]{1,0:T(8,128)(2,1)} %get-tuple-element.41), channel_id=1, source_target_pairs={{0,64},{64,128},{128,192},{192,0},{1,65},{65,129},{129,193},{193,1... | collective-permute-start | bytes 3538952 | tf_op jit(solution)/shard_map/ppermute | solution.py:23
  161.3 37.1 %collective-permute-start.24 = (bf16[288,2048]{1,0:T(8,128)(2,1)}, bf16[288,2048]{1,0:T(8,128)(2,1)}, u32[]{:S(2)}, u32[]{:S(2)}) collective-permute-start(bf16[288,2048]{1,0:T(8,128)(2,1)} %get-tuple-element.46), channel_id=1, source_target_pairs={{0,192},{64,0},{128,64},{192,128},{1,193},{65,1},{129,65},{193,129... | collective-permute-start | bytes 3538952 | tf_op jit(solution)/shard_map/ppermute | solution.py:23
  164.1 50.1 %collective-permute-start.22 = (bf16[288,2048]{1,0:T(8,128)(2,1)}, bf16[288,2048]{1,0:T(8,128)(2,1)}, u32[]{:S(2)}, u32[]{:S(2)}) collective-permute-start(bf16[288,2048]{1,0:T(8,128)(2,1)} %get-tuple-element.42), channel_id=1, source_target_pairs={{0,192},{64,0},{128,64},{192,128},{1,193},{65,1},{129,65},{193,129... | collective-permute-start | bytes 3538952 | tf_op jit(solution)/shard_map/ppermute | solution.py:23
  192.5 27.6 %collective-permute-start.21 = (bf16[288,2048]{1,0:T(8,128)(2,1)}, bf16[288,2048]{1,0:T(8,128)(2,1)}, u32[]{:S(2)}, u32[]{:S(2)}) collective-permute-start(bf16[288,2048]{1,0:T(8,128)(2,1)} %add_convert_fusion.1), channel_id=1, source_target_pairs={{0,64},{64,128},{128,192},{192,0},{1,65},{65,129},{129,193},{193,1... | collective-permute-start | bytes 3538952 | tf_op jit(solution)/shard_map/ppermute | solution.py:23
  192.5 54.9 %all-to-all-start.1 = ((bf16[8,96,2176]{2,1,0:T(8,128)(2,1)}), bf16[8,96,2176]{2,1,0:T(8,128)(2,1)S(1)}, u32[]{:S(2)}, u32[]{:S(2)}) async-start(bf16[8,96,2176]{2,1,0:T(8,128)(2,1)} %get-tuple-element.27), calls=%async_computation.1 | async-start | bytes 6684672 | tf_op jit(solution)/shard_map/all_to_all | solution.py:351
  197.9 47.4 %collective-permute-start.23 = (bf16[288,2048]{1,0:T(8,128)(2,1)}, bf16[288,2048]{1,0:T(8,128)(2,1)S(1)}, u32[]{:S(2)}, u32[]{:S(2)}) collective-permute-start(bf16[288,2048]{1,0:T(8,128)(2,1)} %get-tuple-element.44), channel_id=1, source_target_pairs={{0,64},{64,128},{128,192},{192,0},{1,65},{65,129},{129,193},{193,1... | collective-permute-start | bytes 3538952 | tf_op jit(solution)/shard_map/ppermute | solution.py:23
  200.6 44.7 %collective-permute-start.25 = (bf16[288,2048]{1,0:T(8,128)(2,1)S(1)}, bf16[288,2048]{1,0:T(8,128)(2,1)S(1)}, u32[]{:S(2)}, u32[]{:S(2)}) collective-permute-start(bf16[288,2048]{1,0:T(8,128)(2,1)S(1)} %add_convert_fusion), channel_id=1, source_target_pairs={{0,192},{64,0},{128,64},{192,128},{1,193},{65,1},{129,65},{193,129... | collective-permute-start | bytes 3538952 | tf_op jit(solution)/shard_map/ppermute | solution.py:23
  264.1 6.6 %collective-permute-start.18 = (bf16[32,4224]{1,0:T(8,128)(2,1)S(1)}, bf16[32,4224]{1,0:T(8,128)(2,1)S(1)}, u32[]{:S(2)}, u32[]{:S(2)}) collective-permute-start(bf16[32,4224]{1,0:T(8,128)(2,1)S(1)} %add_convert_fusion.3), channel_id=1, source_target_pairs={{0,2},{2,4},{4,6},{6,8},{8,10},{10,12},{12,14},{14,0},{1,3},{3,5},... | collective-permute-start | bytes 811016 | tf_op jit(solution)/shard_map/ppermute | solution.py:23
  270.8 10.7 %collective-permute-start.19 = (bf16[32,4224]{1,0:T(8,128)(2,1)S(1)}, bf16[32,4224]{1,0:T(8,128)(2,1)S(1)}, u32[]{:S(2)}, u32[]{:S(2)}) collective-permute-start(bf16[32,4224]{1,0:T(8,128)(2,1)S(1)} %add_convert_fusion.2), channel_id=1, source_target_pairs={{0,2},{2,4},{4,6},{6,8},{8,10},{10,12},{12,14},{14,0},{1,3},{3,5},... | collective-permute-start | bytes 811016 | tf_op jit(solution)/shard_map/ppermute | solution.py:23
  273.5 8.1 %collective-permute-start.16 = (bf16[32,4224]{1,0:T(8,128)(2,1)S(1)}, bf16[32,4224]{1,0:T(8,128)(2,1)S(1)}, u32[]{:S(2)}, u32[]{:S(2)}) collective-permute-start(bf16[32,4224]{1,0:T(8,128)(2,1)S(1)} %add_convert_fusion.4), channel_id=1, source_target_pairs={{0,14},{2,0},{4,2},{6,4},{8,6},{10,8},{12,10},{14,12},{1,15},{3,1}... | collective-permute-start | bytes 811016 | tf_op jit(solution)/shard_map/ppermute | solution.py:23
  (34 other events, 287.1 us)
where the time goes:
time: 289 us; the launch traced here: 283 us
  waiting for transfers between devices  157 us (54%)
  starting transfers between devices  51.4 us (18%)
  Pallas kernels  36.6 us (13%)
  local copies, waits for them, and re-layouts  26.3 us (9%)
  other arithmetic  11.1 us (4%)
    ppermute x26, waiting for transfers between devices, shift(): lax.ppermute(value, axis, [(i, (i + step) % size) for i in range(size)])  157 us
    ppermute x26, starting transfers between devices, shift(): lax.ppermute(value, axis, [(i, (i + step) % size) for i in range(size)])  37.8 us
    pallas_call x1, Pallas kernels, body(): call(functools.partial(expert_kernel, n), [((dests, 2 * cap, width + LANE...  23.4 us
    unnamed x64, local copies, waits for them, and re-layouts  14.7 us
    all_to_all x1, starting transfers between devices, body(): arrived = lax.all_to_all(send, ('x', 'c'), 0, 0, tiled=True)  8.16 us
    pallas_call x1, Pallas kernels, body(): call(functools.partial(combine_kernel, top), [((tok_count, wide), BF16)]...  6.09 us
  transfers between devices with their start and end apart: 28, of which 18 were waited for; matrix products, arithmetic and copies ran while one was open for 9% of the time, Pallas kernels for 2%

commit v1 on v0

v1 whole, which is shorter than its diff:
```python
import functools

import jax
import jax.numpy as jnp
from jax import lax
from jax.experimental import pallas as pl
from jax.experimental.pallas import tpu as pltpu
from jax.sharding import Mesh
from jax.sharding import PartitionSpec as P

F32 = jnp.float32
BF16 = jnp.bfloat16
LANES = 128
TILE = 512
PIECES = 5
PLACES = ((0, 0), (0, 3), (1, 0), (1, 3), (2, 0), (2, 3), (3, 0), (4, 0))
MIB = 56
COST = {"pack": 0, "touch2": 0, "weights": 10, "select": 0, "merge": 80, "combine": 0, "combine_cot": 0, "forward": 1, "backward": 1, "final": 0, "touch": 10}
VMEM = pl.BlockSpec(memory_space=pltpu.VMEM)
SMEM = pl.BlockSpec(memory_space=pltpu.SMEM)
ANY = pl.BlockSpec(memory_space=pl.ANY)


def shift(value, axis, step):
    size = lax.axis_size(axis)
    return lax.ppermute(value, axis, [(i, (i + step) % size) for i in range(size)])


def dot(left, right, left_dim, right_dim):
    return lax.dot_general(
        left, right, (((left_dim,), (right_dim,)), ((), ())), preferred_element_type=F32
    )


def call(kernel, outs, in_specs, out_specs, scratch, flops, bytes_accessed, mib, name):
    return pl.pallas_call(
        kernel,
        out_shape=[jax.ShapeDtypeStruct(s, d) for s, d in outs],
        in_specs=in_specs,
        out_specs=out_specs,
        scratch_shapes=scratch,
        compiler_params=pltpu.CompilerParams(vmem_limit_bytes=mib * 1024 * 1024),
        cost_estimate=pl.CostEstimate(
            flops=COST[name] * 10**9, bytes_accessed=0, transcendentals=0
        ),
        name=name,
    )


def split3(value):
    high = value.astype(BF16)
    rest = value - high.astype(F32)
    middle = rest.astype(BF16)
    low = (rest - middle.astype(F32)).astype(BF16)
    return high, middle, low


def pack_kernel(tokens, ids, gates, grads, packed):
    width = tokens.shape[1]
    top = ids.shape[0]
    row = lax.broadcasted_iota(jnp.int32, (top, LANES), 0)
    lane = lax.broadcasted_iota(jnp.int32, (top, LANES), 1)
    fields = (ids[...].astype(F32).astype(BF16),) + split3(gates[...])
    tail = jnp.zeros((tokens.shape[0], LANES), F32)
    for index, field in enumerate(fields):
        place = (lane == row + index * top).astype(F32).astype(BF16)
        tail = tail + dot(field, place, 0, 0)
    packed[:, :width] = tokens[...]
    packed[:, width : width + LANES] = tail.astype(BF16)
    packed[:, width + LANES :] = grads[...]


def weights_kernel(gate_up, down, own):
    half = own.shape[0] // 6
    for part in range(2):
        units = slice(part * half, (part + 1) * half)
        first = 3 * part * half
        for kind in range(2):
            rows = slice(first + kind * half, first + (kind + 1) * half)
            own[rows, :] = gate_up[0, units, kind, :]
        own[first + 2 * half : first + 3 * half, :] = down[0, units, :]


def gather_blocks(blocks, held):
    first = 0
    for block in blocks:
        held[first : first + block.shape[0], :] = block[...]
        first += block.shape[0]


def select_kernel(top, dests, cap, z_index, *refs):
    blocks = refs[:5]
    send, pick_out, gate_out, place_out, held = refs[-5:]
    width = send.shape[2]
    count = held.shape[0]
    gather_blocks(blocks, held)
    info = held[:, width : width + LANES].astype(F32).T
    ids = info[:top]
    gates = info[top : 2 * top] + info[2 * top : 3 * top] + info[3 * top : 4 * top]
    order = lax.broadcasted_iota(jnp.int32, (top, count), 0).astype(F32)
    base = (z_index[0] * 2).astype(F32)
    marks, gate_rows, place_rows = [], [], []
    for dest in range(dests):
        expert = base + float((dest // 2) * 16 + dest % 2)
        chosen = ids == expert
        marks.append(jnp.sum(jnp.where(chosen, 1.0, 0.0), 0, keepdims=True))
        gate_rows.append(jnp.sum(jnp.where(chosen, gates, 0.0), 0, keepdims=True))
        place_rows.append(jnp.sum(jnp.where(chosen, order, 0.0), 0, keepdims=True))
    mark = jnp.concatenate(marks, 0)
    before = lax.broadcasted_iota(jnp.int32, (count, count), 0) < lax.broadcasted_iota(
        jnp.int32, (count, count), 1
    )
    rank = dot(mark.astype(BF16), before.astype(F32).astype(BF16), 1, 0)
    rank = jnp.where(mark > 0, rank, -1.0)
    slot = lax.broadcasted_iota(jnp.int32, (cap, count), 0).astype(F32)
    slot_gates = []
    for dest in range(dests):
        span = slice(dest * cap, (dest + 1) * cap)
        hit = rank[dest : dest + 1] == slot
        pick_out[span, :] = jnp.where(hit, 1.0, 0.0).astype(BF16)
        slot_gate = jnp.sum(jnp.where(hit, gate_rows[dest], 0.0), 1, keepdims=True)
        slot_place = jnp.sum(jnp.where(hit, place_rows[dest], 0.0), 1, keepdims=True)
        gate_out[span, :] = jnp.broadcast_to(slot_gate, (cap, LANES))
        place_out[span, :] = jnp.broadcast_to(slot_place, (cap, LANES))
        slot_gates.append(slot_gate)
    slot_gate = jnp.concatenate(slot_gates, 0)

    def columns(step, carry):
        span = pl.ds(pl.multiple_of(step * TILE, TILE), TILE)
        tok = dot(pick_out[...], held[:, span], 1, 0).astype(BF16)
        send[:, :cap, span] = tok.reshape(dests, cap, TILE)
        second = pl.ds(pl.multiple_of(step * TILE + width + LANES, LANES), TILE)
        cot = slot_gate * dot(pick_out[...], held[:, second], 1, 0)
        send[:, cap:, span] = cot.astype(BF16).reshape(dests, cap, TILE)
        return carry

    lax.fori_loop(0, width // TILE, columns, 0)


def load(pieces, places, weights, sems):
    half = pieces[-1].shape[0] // 3
    copies = []
    for index, (number, first) in enumerate(places):
        group = []
        for slot, (kind, weight) in enumerate(weights):
            copy = pltpu.make_async_copy(
                pieces[number].at[pl.ds(first * half + kind * half, half), :],
                weight.at[pl.ds(index * half, half), :],
                sems.at[index * len(weights) + slot],
            )
            copy.start()
            group.append(copy)
        copies.append(group)
    return copies


def wait_all(copies):
    for group in copies:
        for copy in group:
            copy.wait()


def hidden_parts(gate_pre, up_pre, hidden_cot):
    sigma = jax.nn.sigmoid(gate_pre)
    gate_cot = hidden_cot * up_pre * sigma * (1.0 + gate_pre * (1.0 - sigma))
    return gate_cot, hidden_cot * (gate_pre * sigma)


def fold(value):
    wide = jnp.concatenate([value, jnp.zeros((value.shape[0], 64), F32)], 1)
    return wide[:, :LANES] + wide[:, LANES:]


def forward_kernel(arrived, *refs):
    pieces = refs[:PIECES]
    gate_all, up_all, hid, result, gcot, ucot, score, grad_0, grad_1 = refs[PIECES : PIECES + 9]
    hid_far, lefts, w_gate, w_up, w_down, sems = refs[PIECES + 9 :]
    dests, double, width = arrived.shape
    cap = double // 2
    count = dests * cap
    half = grad_0.shape[0] // 3
    copies = load(pieces, PLACES, ((0, w_gate), (1, w_up), (2, w_down)), sems)
    rows = arrived[:, :cap, :].reshape(count, width)
    shards = len(PLACES) // 2
    hidden = []
    for shard in range(shards):
        wait_all(copies[2 * shard : 2 * shard + 2])
        span = slice(2 * shard * half, 2 * (shard + 1) * half)
        gate_pre = dot(rows, w_gate[span, :], 1, 1)
        up_pre = dot(rows, w_up[span, :], 1, 1)
        value = (gate_pre * jax.nn.sigmoid(gate_pre) * up_pre).astype(BF16)
        if shard < shards - 1:
            gate_all[shard], up_all[shard], hid[shard] = gate_pre, up_pre, value
            hidden.append(hid.at[shard])
    hid_far[...] = value
    hidden.append(hid_far)
    hidden_cot = dot(arrived[:, cap:, :].reshape(count, width), w_down[span, :], 1, 1)
    gate_cot, up_cot = hidden_parts(gate_pre, up_pre, hidden_cot)
    gcot[...] = gate_cot.astype(BF16)
    ucot[...] = up_cot.astype(BF16)
    score[...] = fold(value.astype(F32) * hidden_cot)
    lefts[0] = gate_cot.T.astype(BF16)
    lefts[1] = up_cot.T.astype(BF16)
    lefts[2] = value.astype(F32).T.astype(BF16)
    write_grads(arrived, lefts, (grad_0, grad_1))

    def columns(step, carry):
        span = pl.ds(pl.multiple_of(step * TILE, TILE), TILE)
        out = jnp.zeros((count, TILE), F32)
        for shard, value in enumerate(hidden):
            units = slice(2 * shard * half, 2 * (shard + 1) * half)
            out = out + dot(value[...], w_down[units, span], 1, 0)
        result[:, :, span] = out.astype(BF16).reshape(dests, cap, TILE)
        return carry

    lax.fori_loop(0, width // TILE, columns, 0)


def write_grads(arrived, lefts, pieces):
    dests, double, width = arrived.shape
    cap = double // 2
    count = dests * cap
    half = pieces[0].shape[0] // 3

    def columns(step, carry):
        span = pl.ds(pl.multiple_of(step * TILE, TILE), TILE)
        rows = arrived[:, :cap, span].reshape(count, TILE)
        cots = arrived[:, cap:, span].reshape(count, TILE)
        for kind, right in enumerate((rows, rows, cots)):
            grad = dot(lefts[kind], right, 1, 0).astype(BF16)
            for index, piece in enumerate(pieces):
                piece[kind * half : (kind + 1) * half, span] = grad[
                    index * half : (index + 1) * half
                ]
        return carry

    lax.fori_loop(0, width // TILE, columns, 0)


def backward_kernel(arrived, gate_all, up_all, hid, gcot_far, ucot_far, score_far, *refs):
    pieces = refs[:PIECES]
    near = len(PLACES) - 2
    result = refs[PIECES]
    grads = refs[PIECES + 1 : PIECES + 1 + near]
    gcot, ucot, lefts, w_gate, w_up, w_down, sems = refs[PIECES + 1 + near :]
    dests, double, width = arrived.shape
    cap = double // 2
    count = dests * cap
    half = grads[0].shape[0] // 3
    copies = load(pieces, PLACES[:near], ((2, w_down),), sems.at[pl.ds(0, near)])
    others = load(pieces, PLACES, ((0, w_gate), (1, w_up)), sems.at[pl.ds(near, 2 * near + 4)])
    cots = arrived[:, cap:, :].reshape(count, width)
    score = score_far[...]
    for shard in range(near // 2):
        wait_all(copies[2 * shard : 2 * shard + 2])
        span = slice(2 * shard * half, 2 * (shard + 1) * half)
        hidden_cot = dot(cots, w_down[span, :], 1, 1)
        hidden = hid[shard].astype(F32)
        gate_cot, up_cot = hidden_parts(gate_all[shard], up_all[shard], hidden_cot)
        gcot[shard] = gate_cot.astype(BF16)
        ucot[shard] = up_cot.astype(BF16)
        lefts[0, span, :] = gate_cot.T.astype(BF16)
        lefts[1, span, :] = up_cot.T.astype(BF16)
        lefts[2, span, :] = hidden.T.astype(BF16)
        score = score + fold(hidden * hidden_cot)
    total = jnp.sum(score, 1, keepdims=True)
    lane = lax.broadcasted_iota(jnp.int32, (count, LANES), 1)
    high, middle, low = (part.astype(F32) for part in split3(total))
    tail = jnp.where(lane == 0, high, jnp.where(lane == 1, middle, jnp.where(lane == 2, low, 0.0)))
    result[:, :, width:] = tail.astype(BF16).reshape(dests, cap, LANES)
    write_grads(arrived, lefts, grads)
    wait_all(others)

    def columns(step, carry):
        span = pl.ds(pl.multiple_of(step * TILE, TILE), TILE)
        first = half * near
        dx = dot(gcot_far[...], w_gate[first:, span], 1, 0)
        dx = dx + dot(ucot_far[...], w_up[first:, span], 1, 0)
        for shard in range(near // 2):
            units = slice(2 * shard * half, 2 * (shard + 1) * half)
            dx = dx + dot(gcot[shard], w_gate[units, span], 1, 0)
            dx = dx + dot(ucot[shard], w_up[units, span], 1, 0)
        result[:, :, span] = dx.astype(BF16).reshape(dests, cap, TILE)
        return carry

    lax.fori_loop(0, width // TILE, columns, 0)


def spread_blocks(blocks, value, span):
    first = 0
    for block in blocks:
        block[:, span] = value[first : first + block.shape[0]]
        first += block.shape[0]


def combine_kernel(back, pick, slot_gate, joined, *blocks):
    del joined
    dests, cap, width = back.shape

    def columns(step, carry):
        span = pl.ds(pl.multiple_of(step * TILE, TILE), TILE)
        out = back[:, :, span].reshape(dests * cap, TILE).astype(F32)
        weighted = (slot_gate[:, :1] * out).astype(BF16)
        spread_blocks(blocks, dot(pick[...], weighted, 0, 0).astype(BF16), span)
        return carry

    lax.fori_loop(0, width // TILE, columns, 0)


def combine_cot_kernel(top, back, pick, slot_gate, slot_place, *blocks):
    dests, cap, wide = back.shape
    width = wide - LANES
    count = dests * cap
    gate = slot_gate[:, :1]

    def columns(step, carry):
        span = pl.ds(pl.multiple_of(step * TILE, TILE), TILE)
        dx = back[:, :, span].reshape(count, TILE)
        spread_blocks(blocks, dot(pick[...], dx, 0, 0).astype(BF16), span)
        return carry

    lax.fori_loop(0, width // TILE, columns, 0)
    tail = back[:, :, width:].reshape(count, LANES).astype(F32)
    total = jnp.sum(tail, 1, keepdims=True) / jnp.where(gate > 0, gate, 1.0)
    lane = lax.broadcasted_iota(jnp.int32, (count, LANES), 1).astype(F32)
    spread = jnp.zeros((count, LANES), F32)
    for index, part in enumerate(split3(total)):
        spread = jnp.where(lane == slot_place[...] + float(index * top), part.astype(F32), spread)
    tail = dot(pick[...], spread.astype(BF16), 0, 0).astype(BF16)
    spread_blocks(blocks, tail, slice(width, wide))


def along(value, sign):
    size = lax.axis_size("z")
    pairs = []
    for z in range(size):
        pairs.append((2 * z, 2 * ((z + sign) % size)))
        pairs.append((2 * z + 1, 2 * ((z - sign) % size) + 1))
    return lax.ppermute(value, ("z", "c"), pairs)


def swap(value):
    return lax.ppermute(value, "c", [(0, 1), (1, 0)])


def ring_gather(block, pair):
    far = lax.axis_size("z") // 2
    blocks = [block]
    moving = pair
    for step in range(far):
        moving = along(moving if step < far - 1 else moving[: block.shape[0]], 1)
        blocks.append(moving)
    return blocks


def ring_reduce(blocks):
    rows = blocks[0].shape[0]
    far = len(blocks) - 1
    arrived = [along(blocks[step], -step).astype(F32) for step in range(1, far + 1)]
    both = sum(arrived[:-1])
    other = swap(both[rows:].astype(BF16))
    return blocks[0].astype(F32) + both[:rows] + arrived[-1] + other.astype(F32)


def merge_kernel(first_0, relayed_0, second_0, first_1, relayed_1, second_1, joined_0, joined_1):
    rows = first_0.shape[0]
    joined_0[:rows, :] = (first_0[...].astype(F32) + relayed_0[...].astype(F32)).astype(BF16)
    joined_0[rows:, :] = second_0[...]
    joined_1[:rows, :] = (first_1[...].astype(F32) + relayed_1[...].astype(F32)).astype(BF16)
    joined_1[rows:, :] = second_1[...]


def touch_kernel(left, right, left_out, right_out):
    del left, right, left_out, right_out


def touch(left, right, name):
    return pl.pallas_call(
        touch_kernel,
        out_shape=[jax.ShapeDtypeStruct(v.shape, v.dtype) for v in (left, right)],
        in_specs=[ANY] * 2,
        out_specs=[ANY] * 2,
        input_output_aliases={0: 0, 1: 1},
        cost_estimate=pl.CostEstimate(
            flops=COST[name] * 10**9, bytes_accessed=0, transcendentals=0
        ),
        name=name,
    )(left, right)


def final_kernel(own_0, own_1, before, after, gate_up_grad, down_grad):
    rows = own_0.shape[0]
    half = rows // 3
    for side, own in ((0, own_0), (1, own_1)):
        units = slice(side * half, (side + 1) * half)
        for kind in range(3):
            span = slice(kind * half, (kind + 1) * half)
            up = slice(side * rows + kind * half, side * rows + (kind + 1) * half)
            down = slice((1 - side) * rows + kind * half, (1 - side) * rows + (kind + 1) * half)
            total = own[span, :].astype(F32) + before[up, :].astype(F32)
            total = total + after[down, :].astype(F32)
            if kind < 2:
                gate_up_grad[0, units, kind, :] = total
            else:
                down_grad[0, units, :] = total


def body(tokens, expert_ids, route_gates, gate_up, down_weight, out_grad):
    tok_count, width = tokens.shape
    top = expert_ids.shape[1]
    z_size = lax.axis_size("z")
    dests = lax.axis_size("x") * 2
    cap = 6 * z_size
    count = dests * cap
    held = tok_count * z_size
    units = gate_up.shape[1]
    half = units // 2
    wide = width + LANES
    n = 8
    full = n * half

    double = 2 * width + LANES
    (packed,) = call(
        pack_kernel, [((tok_count, double), BF16)], [VMEM] * 4, [VMEM], [], 0, 0, MIB, "pack"
    )(tokens, expert_ids.T, route_gates.T, out_grad)
    pair = jnp.concatenate([packed, swap(packed)], 0)
    pair, gate_up, down_weight = lax.optimization_barrier((pair, gate_up, down_weight))
    blocks = ring_gather(packed, pair)
    three = 3 * half
    (own,) = call(
        weights_kernel,
        [((2 * three, width), BF16)],
        [VMEM] * 2,
        [VMEM],
        [],
        0,
        0,
        MIB,
        "weights",
    )(gate_up, down_weight)
    before = shift(own, "dp", 1)
    after = shift(own, "dp", -1)
    z_index = lax.axis_index("z").astype(jnp.int32).reshape(1)
    rows_type = ((dests, cap, width), BF16)
    pick_flops = 2 * count * held * width
    send, pick, slot_gate, slot_place = call(
        functools.partial(select_kernel, top, dests, cap),
        [((dests, 2 * cap, width), BF16), ((count, held), BF16)] + [((count, LANES), F32)] * 2,
        [SMEM] + [VMEM] * len(blocks),
        [VMEM] * 4,
        [pltpu.VMEM((held, double), BF16)],
        pick_flops,
        3 * 10**6,
        MIB,
        "select",
    )(z_index, *blocks)
    before, after, _ = lax.optimization_barrier((before, after, send))
    far_0 = shift(before[:three], "dp", 1)
    far_1 = shift(after[three:], "dp", -1)
    far_0, far_1 = touch(far_0, far_1, "touch")
    pieces = [own, before, after, far_0, far_1]

    arrived = lax.all_to_all(send, ("x", "c"), 0, 0, tiled=True)

    shards = n // 2 - 1
    hidden_type = ((count, units), BF16)
    piece_type = ((3 * half, width), BF16)
    weight = pltpu.VMEM((full, width), BF16)
    gate_all, up_all, hid, result, gcot_f, ucot_f, score_f, far_g0, far_g1 = call(
        forward_kernel,
        [((shards, count, units), F32)] * 2
        + [((shards, count, units), BF16), rows_type, hidden_type, hidden_type]
        + [((count, LANES), F32)]
        + [piece_type] * 2,
        [VMEM] + [ANY] * len(pieces),
        [VMEM] * 9,
        [pltpu.VMEM((count, units), BF16), pltpu.VMEM((3, units, count), BF16)]
        + [weight] * 3
        + [pltpu.SemaphoreType.DMA((3 * n,))],
        1,
        0,
        MIB,
        "forward",
    )(arrived, *pieces)
    result_cot, own_0, own_1, before_g0, before_g1, after_g0, after_g1 = call(
        backward_kernel,
        [((dests, cap, wide), BF16)] + [piece_type] * (n - 2),
        [VMEM] * 7 + [ANY] * len(pieces),
        [VMEM] * (n - 1),
        [pltpu.VMEM((shards, count, units), BF16)] * 2
        + [pltpu.VMEM((3, units * shards, count), BF16)]
        + [weight] * 3
        + [pltpu.SemaphoreType.DMA((3 * n - 2,))],
        1,
        0,
        MIB,
        "backward",
    )(arrived, gate_all, up_all, hid, gcot_f, ucot_f, score_f, *pieces)

    relay_0 = shift(far_g0, "dp", 1)
    relay_1 = shift(far_g1, "dp", -1)

    joined_0, joined_1 = call(
        merge_kernel,
        [((2 * three, width), BF16)] * 2,
        [VMEM] * 6,
        [VMEM] * 2,
        [],
        1,
        0,
        MIB,
        "merge",
    )(after_g0, relay_0, after_g1, before_g1, relay_1, before_g0)
    got_before = shift(joined_0, "dp", 1)
    got_after = shift(joined_1, "dp", -1)
    got_before, got_after = touch(got_before, got_after, "touch2")
    gate_up_grad, down_grad = call(
        final_kernel,
        [(gate_up.shape, F32), (down_weight.shape, F32)],
        [VMEM] * 4,
        [VMEM] * 2,
        [],
        0,
        0,
        MIB,
        "final",
    )(own_0, own_1, got_before, got_after)

    back = lax.all_to_all(result, ("x", "c"), 0, 0, tiled=True)
    parts = call(
        combine_kernel,
        [((b.shape[0], width), BF16) for b in blocks],
        [VMEM] * 3 + [ANY],
        [VMEM] * len(blocks),
        [],
        pick_flops,
        3 * 10**6,
        MIB,
        "combine",
    )(back, pick, slot_gate, joined_0)
    moe_out = ring_reduce(list(parts)).astype(BF16)
    back_cot = lax.all_to_all(result_cot, ("x", "c"), 0, 0, tiled=True)
    parts = call(
        functools.partial(combine_cot_kernel, top),
        [((b.shape[0], wide), BF16) for b in blocks],
        [VMEM] * 4,
        [VMEM] * len(blocks),
        [],
        pick_flops,
        3 * 10**6,
        MIB,
        "combine_cot",
    )(back_cot, pick, slot_gate, slot_place)
    summed = ring_reduce(list(parts))
    token_grad = summed[:, :width].astype(BF16)
    tail = summed[:, width:]
    gate_grad = tail[:, :top] + tail[:, top : 2 * top] + tail[:, 2 * top : 3 * top]
    return moe_out, gate_grad, token_grad, gate_up_grad, down_grad


def solution(mesh):
    wide = Mesh(mesh.devices.reshape(4, 4, 8, 2), ("dp", "x", "z", "c"))
    expert = ("x", "z", "c")
    every = ("dp",) + expert
    in_specs = (
        P(every, None),
        P(every, None),
        P(every, None),
        P(expert, "dp", None, None),
        P(expert, "dp", None),
        P(every, None),
    )
    out_specs = (
        P(every, None),
        P(every, None),
        P(every, None),
        P(expert, "dp", None, None),
        P(expert, "dp", None),
    )
    return jax.shard_map(body, mesh=wide, in_specs=in_specs, out_specs=out_specs, check_vma=False)
```

time: 289 us -> 235 us (0.81); the launches traced: 283 us -> 234 us
  waiting for transfers between devices: 157 us -> 92.2 us
  Pallas kernels: 36.6 us -> 68.1 us
  local copies, waits for them, and re-layouts: 26.3 us -> 9.14 us
  starting transfers between devices: 51.4 us -> 61.9 us
  other arithmetic: 11.1 us -> 2.03 us
    ppermute x26 -> x8, waiting for transfers between devices: 157 us -> 46.1 us  [shift(): lax.ppermute(value, axis, [(i, (i + step) % size) for i in range(size)])]
    ppermute x0 -> x15, waiting for transfers between devices: none -> 45 us  [the longest x12 42.9 us: along(): return lax.ppermute(value, ('z', 'c'), pairs)]
    ppermute x0 -> x15, starting transfers between devices: none -> 34.3 us  [the longest x12 22.8 us: along(): return lax.ppermute(value, ('z', 'c'), pairs)]
    pallas_call x3 -> x10, Pallas kernels: 31.4 us -> 62.9 us  [the longest x1 18.2 us: body(): call(backward_kernel, [((dests, cap, wide), BF16)] + [piece_type] * (n -...]
    ppermute x26 -> x8, starting transfers between devices: 37.8 us -> 9.63 us  [shift(): lax.ppermute(value, axis, [(i, (i + step) % size) for i in range(size)])]
    unnamed x64 -> x25, local copies, waits for them, and re-layouts: 14.7 us -> 5.64 us
    slice x7 -> x6, local copies, waits for them, and re-layouts: 11.5 us -> 3.5 us  [the longest x1 1.39 us: body(): far_1 = shift(after[three:], 'dp', -1)]
    all_to_all x0 -> x1, starting transfers between devices: none -> 5.37 us  [body(): back_cot = lax.all_to_all(result_cot, ('x', 'c'), 0, 0, tiled=True)]
  transfers between devices with their start and end apart: 28 -> 26, of which waited for: 18 -> 18; matrix products, arithmetic and copies ran while one was open for 9% -> 2% of each run, Pallas kernels for 2% -> 19%
where the time goes in v1:
time: 235 us; the launch traced here: 234 us
  waiting for transfers between devices  92.2 us (39%)
  Pallas kernels  68.1 us (29%)
  starting transfers between devices  61.9 us (26%)
  local copies, waits for them, and re-layouts  9.14 us (4%)
    ppermute x8, waiting for transfers between devices, shift(): lax.ppermute(value, axis, [(i, (i + step) % size) for i in range(size)])  46.1 us
    ppermute x12, waiting for transfers between devices, along(): return lax.ppermute(value, ('z', 'c'), pairs)  42.9 us
    ppermute x12, starting transfers between devices, along(): return lax.ppermute(value, ('z', 'c'), pairs)  22.8 us
    pallas_call x1, Pallas kernels, body(): call(backward_kernel, [((dests, cap, wide), BF16)] + [piece_type] * (n -...  18.2 us
    pallas_call x1, Pallas kernels, body(): call(forward_kernel, [((shards, count, units), F32)] * 2 + [((shards, cou...  16 us
    ppermute x3, starting transfers between devices, swap(): return lax.ppermute(value, 'c', [(0, 1), (1, 0)])  11.4 us
    ppermute x8, starting transfers between devices, shift(): lax.ppermute(value, axis, [(i, (i + step) % size) for i in range(size)])  9.63 us
    all_to_all x1, starting transfers between devices, body(): arrived = lax.all_to_all(send, ('x', 'c'), 0, 0, tiled=True)  8.03 us
  transfers between devices with their start and end apart: 26, of which 18 were waited for; matrix products, arithmetic and copies ran while one was open for 2% of the time, Pallas kernels for 19%

profile of v1, /device:TPU:1, one launch (start us, length us, event | category | flops | bytes accessed | tf_op | source)
XLA Modules:
  0.0 234.1 jit_solution(3020301674982272162)
XLA Ops:
  8.2 3.9 %collective-permute-start.1 = (bf16[64,4224]{1,0:T(8,128)(2,1)S(1)}, bf16[64,4224]{1,0:T(8,128)(2,1)S(1)}, u32[]{:S(2)}, u32[]{:S(2)}) collective-permute-start(bf16[64,4224]{1,0:T(8,128)(2,1)S(1)} %pad_maximum_fusion), channel_id=1, source_target_pairs={{0,2},{1,15},{2,4},{3,1},{4,6},{5,3},{6,8},{7,5},{8,10},{9,7},{10,... | collective-permute-start | bytes 1622024 | tf_op jit(solution)/shard_map/ppermute | solution.py:339
  12.1 6.5 %weights.1.refs_0_ = bf16[576,2048]{1,0:T(8,128)(2,1)} custom-call(bf16[1,192,2,2048]{3,2,1,0:T(2,128)(2,1)} %gate_up, bf16[1,192,2048]{2,1,0:T(8,128)(2,1)} %down), custom_call_target="tpu_custom_call" | custom-call | flops 10000000000 | tf_op jit(solution)/shard_map/weights/pallas_call | solution.py:430
  22.1 7.9 %collective-permute-done.2.refs_2_ = bf16[64,4224]{1,0:T(8,128)(2,1)S(1)} collective-permute-done((bf16[64,4224]{1,0:T(8,128)(2,1)S(1)}, bf16[64,4224]{1,0:T(8,128)(2,1)S(1)}, u32[]{:S(2)}, u32[]{:S(2)}) %collective-permute-start.2) | collective-permute-done | bytes 540704 | tf_op jit(solution)/shard_map/ppermute | solution.py:339
  31.9 6.7 %collective-permute-done.3.refs_3_ = bf16[64,4224]{1,0:T(8,128)(2,1)S(1)} collective-permute-done((bf16[64,4224]{1,0:T(8,128)(2,1)S(1)}, bf16[64,4224]{1,0:T(8,128)(2,1)S(1)}, u32[]{:S(2)}, u32[]{:S(2)}) %collective-permute-start.3) | collective-permute-done | bytes 540704 | tf_op jit(solution)/shard_map/ppermute | solution.py:339
  41.9 3.4 %collective-permute-done.4.refs_4_ = bf16[32,4224]{1,0:T(8,128)(2,1)S(1)} collective-permute-done((bf16[32,4224]{1,0:T(8,128)(2,1)S(1)}, bf16[32,4224]{1,0:T(8,128)(2,1)S(1)}, u32[]{:S(2)}, u32[]{:S(2)}) %collective-permute-start.4) | collective-permute-done | bytes 270368 | tf_op jit(solution)/shard_map/ppermute | solution.py:339
  46.0 5.2 %select.1 = (bf16[8,96,2048]{2,1,0:T(8,128)(2,1)}, bf16[384,256]{1,0:T(8,128)(2,1)}, f32[384,128]{1,0:T(8,128)}, f32[384,128]{1,0:T(8,128)}) custom-call(s32[1]{0:T(128)} %bitcast.z_index, bf16[32,4224]{1,0:T(8,128)(2,1)} %pack.1.refs_0_, bf16[64,4224]{1,0:T(8,128)(2,1)} %copy-done.4, bf16[64,4224]{1,0:T(8,128)(2,1)} %copy-done.5, ...), custom_call_target="tpu_custom_call" | custom-call | tf_op jit(solution)/shard_map/select/pallas_call | solution.py:446
  51.2 8.0 %all-to-all-start = ((bf16[8,96,2048]{2,1,0:T(8,128)(2,1)}), bf16[8,96,2048]{2,1,0:T(8,128)(2,1)S(1)}, u32[]{:S(2)}, u32[]{:S(2)}) async-start(bf16[8,96,2048]{2,1,0:T(8,128)(2,1)} %get-tuple-element.49), calls=%async_computation | async-start | bytes 6291456 | tf_op jit(solution)/shard_map/all_to_all | solution.py:463
  59.3 10.6 %collective-permute-done.6.refs_2_ = bf16[576,2048]{1,0:T(8,128)(2,1)} collective-permute-done((bf16[576,2048]{1,0:T(8,128)(2,1)}, bf16[576,2048]{1,0:T(8,128)(2,1)}, u32[]{:S(2)}, u32[]{:S(2)}) %collective-permute-start.6) | collective-permute-done | bytes 2359328 | tf_op jit(solution)/shard_map/ppermute | solution.py:26
  77.6 25.1 %collective-permute-done.8.right = bf16[288,2048]{1,0:T(8,128)(2,1)} collective-permute-done((bf16[288,2048]{1,0:T(8,128)(2,1)S(1)}, bf16[288,2048]{1,0:T(8,128)(2,1)}, u32[]{:S(2)}, u32[]{:S(2)}) %collective-permute-start.8) | collective-permute-done | bytes 1179680 | tf_op jit(solution)/shard_map/ppermute | solution.py:26
  105.6 16.0 %forward.1 = (f32[3,384,192]{2,1,0:T(8,128)}, f32[3,384,192]{2,1,0:T(8,128)}, bf16[3,384,192]{2,1,0:T(8,128)(2,1)}, bf16[8,48,2048]{2,1,0:T(8,128)(2,1)}, bf16[3...) custom-call(bf16[8,96,2048]{2,1,0:T(8,128)(2,1)} %copy-done, ...), custom_call_target="tpu_custom_call" | custom-call | flops 1000000000 | tf_op jit(solution)/shard_map/forward/pallas_call | solution.py:469
  121.6 4.5 %all-to-all-start.1 = ((bf16[8,48,2048]{2,1,0:T(8,128)(2,1)}), bf16[8,48,2048]{2,1,0:T(8,128)(2,1)S(1)}, u32[]{:S(2)}, u32[]{:S(2)}) async-start(bf16[8,48,2048]{2,1,0:T(8,128)(2,1)} %get-tuple-element.56), calls=%async_computation.1 | async-start | bytes 3145728 | tf_op jit(solution)/shard_map/all_to_all | solution.py:529
  128.8 18.2 %backward.1 = (bf16[8,48,2176]{2,1,0:T(8,128)(2,1)}, bf16[288,2048]{1,0:T(8,128)(2,1)}, bf16[288,2048]{1,0:T(8,128)(2,1)}, bf16[288,2048]{1,0:T(8,128)(2,1)}, bf...) custom-call(bf16[8,96,2048]{2,1,0:T(8,128)(2,1)} %copy-done, ...), custom_call_target="tpu_custom_call" | custom-call | flops 1000000000 | tf_op jit(solution)/shard_map/backward/pallas_call | solution.py:485
  148.2 5.4 %all-to-all-start.2 = ((bf16[8,48,2176]{2,1,0:T(8,128)(2,1)}), bf16[8,48,2176]{2,1,0:T(8,128)(2,1)}, u32[]{:S(2)}, u32[]{:S(2)}) async-start(bf16[8,48,2176]{2,1,0:T(8,128)(2,1)} %get-tuple-element.77), calls=%async_computation.2 | async-start | bytes 3342336 | tf_op jit(solution)/shard_map/all_to_all | solution.py:542
  155.3 5.5 %merge.1 = (bf16[576,2048]{1,0:T(8,128)(2,1)}, bf16[576,2048]{1,0:T(8,128)(2,1)}) custom-call(bf16[288,2048]{1,0:T(8,128)(2,1)} %get-tuple-element.65.first_0, bf16[288,2048]{1,0:T(8,128)(2,1)} %collective-permute-done.9.relayed_0, bf16[288,2048]{1,0:T(8,128)(2,1)} %get-tuple-element.67.second_0, bf16[288,2048]{1,0:T(8,128)(2,1)} %get-tuple-element.68.first_1, ...), custom_call_target="tpu_custom_call" | custom-call | flops 80000000000 | tf_op jit(solution)/shard_map/merge/pallas_call | solution.py:503
  160.8 4.0 %combine.1 = (bf16[32,2048]{1,0:T(8,128)(2,1)}, bf16[64,2048]{1,0:T(8,128)(2,1)}, bf16[64,2048]{1,0:T(8,128)(2,1)}, bf16[64,2048]{1,0:T(8,128)(2,1)}, bf16[32,2048]{1,0:T(8,128)(2,1)}) custom-call(bf16[8,48,2048]{2,1,0:T(8,128)(2,1)} %copy-done.2, bf16[384,256]{1,0:T(8,128)(2,1)} %get-tuple-element.57.pick, f32[384,128]{1,0:T(8,128)} %get-tuple-element.58.slot_gate, ...), custom_call_target="tpu_custom_call" | custom-call | tf_op jit(solution)/shard_map/combine/pallas_call | solution.py:530
  164.8 7.0 %collective-permute-start.13 = (bf16[64,2048]{1,0:T(8,128)(2,1)}, bf16[64,2048]{1,0:T(8,128)(2,1)S(1)}, u32[]{:S(2)}, u32[]{:S(2)}) collective-permute-start(bf16[64,2048]{1,0:T(8,128)(2,1)} %get-tuple-element.75), channel_id=1, source_target_pairs={{0,10},{1,7},{2,12},{3,9},{4,14},{5,11},{6,0},{7,13},{8,2},{9,15},... | collective-permute-start | bytes 786440 | tf_op jit(solution)/shard_map/ppermute | solution.py:339
  175.5 4.3 %combine_cot.1 = (bf16[32,2176]{1,0:T(8,128)(2,1)}, bf16[64,2176]{1,0:T(8,128)(2,1)}, bf16[64,2176]{1,0:T(8,128)(2,1)}, bf16[64,2176]{1,0:T(8,128)(2,1)}, bf16[32,2176]{1,0:T(8,128)(2,1)}) custom-call(bf16[8,48,2176]{2,1,0:T(8,128)(2,1)} %all-to-all-done.2.back, bf16[384,256]{1,0:T(8,128)(2,1)} %get-tuple-element.57.pick, ...), custom_call_target="tpu_custom_call" | custom-call | tf_op jit(solution)/shard_map/combine_cot/pallas_call | solution.py:543
  181.6 7.3 %collective-permute-done.13 = bf16[64,2048]{1,0:T(8,128)(2,1)S(1)} collective-permute-done((bf16[64,2048]{1,0:T(8,128)(2,1)}, bf16[64,2048]{1,0:T(8,128)(2,1)S(1)}, u32[]{:S(2)}, u32[]{:S(2)}) %collective-permute-start.13) | collective-permute-done | bytes 262176 | tf_op jit(solution)/shard_map/ppermute | solution.py:339
  189.0 3.4 %collective-permute-done.16 = bf16[64,2176]{1,0:T(8,128)(2,1)S(1)} collective-permute-done((bf16[64,2176]{1,0:T(8,128)(2,1)}, bf16[64,2176]{1,0:T(8,128)(2,1)S(1)}, u32[]{:S(2)}, u32[]{:S(2)}) %collective-permute-start.16) | collective-permute-done | bytes 278560 | tf_op jit(solution)/shard_map/ppermute | solution.py:339
  193.0 9.1 %collective-permute-done.17 = bf16[64,2176]{1,0:T(8,128)(2,1)S(1)} collective-permute-done((bf16[64,2176]{1,0:T(8,128)(2,1)}, bf16[64,2176]{1,0:T(8,128)(2,1)S(1)}, u32[]{:S(2)}, u32[]{:S(2)}) %collective-permute-start.17) | collective-permute-done | bytes 278560 | tf_op jit(solution)/shard_map/ppermute | solution.py:339
  202.1 4.5 %collective-permute-start.19 = (bf16[32,2176]{1,0:T(8,128)(2,1)S(1)}, bf16[32,2176]{1,0:T(8,128)(2,1)S(1)}, u32[]{:S(2)}, u32[]{:S(2)}) collective-permute-start(bf16[32,2176]{1,0:T(8,128)(2,1)S(1)} %copy-done.10), channel_id=1, source_target_pairs={{0,8},{1,9},{2,10},{3,11},{4,12},{5,13},{6,14},{7,15},{8,0},{9,1},... | collective-permute-start | bytes 417800 | tf_op jit(solution)/shard_map/ppermute | solution.py:339
  206.6 4.3 %collective-permute-done.18 = bf16[64,2176]{1,0:T(8,128)(2,1)S(1)} collective-permute-done((bf16[64,2176]{1,0:T(8,128)(2,1)}, bf16[64,2176]{1,0:T(8,128)(2,1)S(1)}, u32[]{:S(2)}, u32[]{:S(2)}) %collective-permute-start.18) | collective-permute-done | bytes 278560 | tf_op jit(solution)/shard_map/ppermute | solution.py:339
  210.8 8.1 %collective-permute-start.15 = (bf16[32,2048]{1,0:T(8,128)(2,1)S(1)}, bf16[32,2048]{1,0:T(8,128)(2,1)S(1)}, u32[]{:S(2)}, u32[]{:S(2)}) collective-permute-start(bf16[32,2048]{1,0:T(8,128)(2,1)S(1)} %slice.82), channel_id=1, source_target_pairs={{0,1},{1,0},{2,3},{3,2},{4,5},{5,4},{6,7},{7,6},{8,9},{9,8},{10,11... | collective-permute-start | bytes 393224 | tf_op jit(solution)/shard_map/ppermute | solution.py:343
  227.7 6.4 %final.1 = (f32[1,192,2,2048]{3,2,1,0:T(2,128)}, f32[1,192,2048]{2,1,0:T(8,128)}) custom-call(bf16[288,2048]{1,0:T(8,128)(2,1)} %get-tuple-element.84.own_0, bf16[288,2048]{1,0:T(8,128)(2,1)} %get-tuple-element.85.own_1, bf16[576,2048]{1,0:T(8,128)(2,1)} %get-tuple-element.87.before, bf16[576,2048]{1,0:T(8,128)(2,1)} %get-tuple-element.88.after), custom_call_target="tpu_custom_call" | custom-call | tf_op jit(solution)/shard_map/final/pallas_call | solution.py:517
  (76 shorter events, 48.0 us)
Async XLA Ops:
  8.2 13.1 %collective-permute-start.1 = (bf16[64,4224]{1,0:T(8,128)(2,1)S(1)}, bf16[64,4224]{1,0:T(8,128)(2,1)S(1)}, u32[]{:S(2)}, u32[]{:S(2)}) collective-permute-start(bf16[64,4224]{1,0:T(8,128)(2,1)S(1)} %pad_maximum_fusion), channel_id=1, source_target_pairs={{0,2},{1,15},{2,4},{3,1},{4,6},{5,3},{6,8},{7,5},{8,10},{9,7},{10,... | collective-permute-start | bytes 1622024 | tf_op jit(solution)/shard_map/ppermute | solution.py:339
  18.6 51.3 %collective-permute-start.6 = (bf16[576,2048]{1,0:T(8,128)(2,1)}, bf16[576,2048]{1,0:T(8,128)(2,1)}, u32[]{:S(2)}, u32[]{:S(2)}) collective-permute-start(bf16[576,2048]{1,0:T(8,128)(2,1)} %weights.1.refs_0_), channel_id=1, source_target_pairs={{0,192},{64,0},{128,64},{192,128},{1,193},{65,1},{129,65},{193,129... | collective-permute-start | bytes 7077896 | tf_op jit(solution)/shard_map/ppermute | solution.py:26
  21.3 52.0 %collective-permute-start.5 = (bf16[576,2048]{1,0:T(8,128)(2,1)}, bf16[576,2048]{1,0:T(8,128)(2,1)}, u32[]{:S(2)}, u32[]{:S(2)}) collective-permute-start(bf16[576,2048]{1,0:T(8,128)(2,1)} %weights.1.refs_0_), channel_id=1, source_target_pairs={{0,64},{64,128},{128,192},{192,0},{1,65},{65,129},{129,193},{193,1... | collective-permute-start | bytes 7077896 | tf_op jit(solution)/shard_map/ppermute | solution.py:26
  21.3 8.7 %collective-permute-start.2 = (bf16[64,4224]{1,0:T(8,128)(2,1)S(1)}, bf16[64,4224]{1,0:T(8,128)(2,1)S(1)}, u32[]{:S(2)}, u32[]{:S(2)}) collective-permute-start(bf16[64,4224]{1,0:T(8,128)(2,1)S(1)} %collective-permute-done.1.refs_1_), channel_id=1, source_target_pairs={{0,2},{1,15},{2,4},{3,1},{4,6},{5,3},{6,8},{7,5},{8,10},{9,7},{10,... | collective-permute-start | bytes 1622024 | tf_op jit(solution)/shard_map/ppermute | solution.py:339
  30.0 8.6 %collective-permute-start.3 = (bf16[64,4224]{1,0:T(8,128)(2,1)S(1)}, bf16[64,4224]{1,0:T(8,128)(2,1)S(1)}, u32[]{:S(2)}, u32[]{:S(2)}) collective-permute-start(bf16[64,4224]{1,0:T(8,128)(2,1)S(1)} %collective-permute-done.2.refs_2_), channel_id=1, source_target_pairs={{0,2},{1,15},{2,4},{3,1},{4,6},{5,3},{6,8},{7,5},{8,10},{9,7},{10,... | collective-permute-start | bytes 1622024 | tf_op jit(solution)/shard_map/ppermute | solution.py:339
  38.6 6.6 %collective-permute-start.4 = (bf16[32,4224]{1,0:T(8,128)(2,1)S(1)}, bf16[32,4224]{1,0:T(8,128)(2,1)S(1)}, u32[]{:S(2)}, u32[]{:S(2)}) collective-permute-start(bf16[32,4224]{1,0:T(8,128)(2,1)S(1)} %slice.51), channel_id=1, source_target_pairs={{0,2},{1,15},{2,4},{3,1},{4,6},{5,3},{6,8},{7,5},{8,10},{9,7},{10,... | collective-permute-start | bytes 811016 | tf_op jit(solution)/shard_map/ppermute | solution.py:339
  51.2 52.7 %all-to-all-start = ((bf16[8,96,2048]{2,1,0:T(8,128)(2,1)}), bf16[8,96,2048]{2,1,0:T(8,128)(2,1)S(1)}, u32[]{:S(2)}, u32[]{:S(2)}) async-start(bf16[8,96,2048]{2,1,0:T(8,128)(2,1)} %get-tuple-element.49), calls=%async_computation | async-start | bytes 6291456 | tf_op jit(solution)/shard_map/all_to_all | solution.py:463
  76.0 26.7 %collective-permute-start.8 = (bf16[288,2048]{1,0:T(8,128)(2,1)S(1)}, bf16[288,2048]{1,0:T(8,128)(2,1)}, u32[]{:S(2)}, u32[]{:S(2)}) collective-permute-start(bf16[288,2048]{1,0:T(8,128)(2,1)S(1)} %slice.42), channel_id=1, source_target_pairs={{0,192},{64,0},{128,64},{192,128},{1,193},{65,1},{129,65},{193,129... | collective-permute-start | bytes 3538952 | tf_op jit(solution)/shard_map/ppermute | solution.py:26
  76.1 27.8 %collective-permute-start.7 = (bf16[288,2048]{1,0:T(8,128)(2,1)S(1)}, bf16[288,2048]{1,0:T(8,128)(2,1)}, u32[]{:S(2)}, u32[]{:S(2)}) collective-permute-start(bf16[288,2048]{1,0:T(8,128)(2,1)S(1)} %slice.41), channel_id=1, source_target_pairs={{0,64},{64,128},{128,192},{192,0},{1,65},{65,129},{129,193},{193,1... | collective-permute-start | bytes 3538952 | tf_op jit(solution)/shard_map/ppermute | solution.py:26
  121.6 25.5 %all-to-all-start.1 = ((bf16[8,48,2048]{2,1,0:T(8,128)(2,1)}), bf16[8,48,2048]{2,1,0:T(8,128)(2,1)S(1)}, u32[]{:S(2)}, u32[]{:S(2)}) async-start(bf16[8,48,2048]{2,1,0:T(8,128)(2,1)} %get-tuple-element.56), calls=%async_computation.1 | async-start | bytes 3145728 | tf_op jit(solution)/shard_map/all_to_all | solution.py:529
  126.1 29.1 %collective-permute-start.9 = (bf16[288,2048]{1,0:T(8,128)(2,1)}, bf16[288,2048]{1,0:T(8,128)(2,1)}, u32[]{:S(2)}, u32[]{:S(2)}) collective-permute-start(bf16[288,2048]{1,0:T(8,128)(2,1)} %get-tuple-element.66), channel_id=1, source_target_pairs={{0,64},{64,128},{128,192},{192,0},{1,65},{65,129},{129,193},{193,1... | collective-permute-start | bytes 3538952 | tf_op jit(solution)/shard_map/ppermute | solution.py:26
  126.4 28.9 %collective-permute-start.10 = (bf16[288,2048]{1,0:T(8,128)(2,1)S(1)}, bf16[288,2048]{1,0:T(8,128)(2,1)}, u32[]{:S(2)}, u32[]{:S(2)}) collective-permute-start(bf16[288,2048]{1,0:T(8,128)(2,1)S(1)} %copy-done.9), channel_id=1, source_target_pairs={{0,192},{64,0},{128,64},{192,128},{1,193},{65,1},{129,65},{193,129... | collective-permute-start | bytes 3538952 | tf_op jit(solution)/shard_map/ppermute | solution.py:26
  148.2 27.2 %all-to-all-start.2 = ((bf16[8,48,2176]{2,1,0:T(8,128)(2,1)}), bf16[8,48,2176]{2,1,0:T(8,128)(2,1)}, u32[]{:S(2)}, u32[]{:S(2)}) async-start(bf16[8,48,2176]{2,1,0:T(8,128)(2,1)} %get-tuple-element.77), calls=%async_computation.2 | async-start | bytes 3342336 | tf_op jit(solution)/shard_map/all_to_all | solution.py:542
  164.8 15.0 %collective-permute-start.11 = (bf16[64,2048]{1,0:T(8,128)(2,1)}, bf16[64,2048]{1,0:T(8,128)(2,1)S(1)}, u32[]{:S(2)}, u32[]{:S(2)}) collective-permute-start(bf16[64,2048]{1,0:T(8,128)(2,1)} %get-tuple-element.73), channel_id=1, source_target_pairs={{0,14},{1,3},{2,0},{3,5},{4,2},{5,7},{6,4},{7,9},{8,6},{9,11},{10,... | collective-permute-start | bytes 786440 | tf_op jit(solution)/shard_map/ppermute | solution.py:339
  164.8 16.8 %collective-permute-start.12 = (bf16[64,2048]{1,0:T(8,128)(2,1)}, bf16[64,2048]{1,0:T(8,128)(2,1)S(1)}, u32[]{:S(2)}, u32[]{:S(2)}) collective-permute-start(bf16[64,2048]{1,0:T(8,128)(2,1)} %get-tuple-element.74), channel_id=1, source_target_pairs={{0,12},{1,5},{2,14},{3,7},{4,0},{5,9},{6,2},{7,11},{8,4},{9,13},{1... | collective-permute-start | bytes 786440 | tf_op jit(solution)/shard_map/ppermute | solution.py:339
  164.8 24.1 %collective-permute-start.13 = (bf16[64,2048]{1,0:T(8,128)(2,1)}, bf16[64,2048]{1,0:T(8,128)(2,1)S(1)}, u32[]{:S(2)}, u32[]{:S(2)}) collective-permute-start(bf16[64,2048]{1,0:T(8,128)(2,1)} %get-tuple-element.75), channel_id=1, source_target_pairs={{0,10},{1,7},{2,12},{3,9},{4,14},{5,11},{6,0},{7,13},{8,2},{9,15},... | collective-permute-start | bytes 786440 | tf_op jit(solution)/shard_map/ppermute | solution.py:339
  171.8 54.5 %collective-permute-start.21 = (bf16[576,2048]{1,0:T(8,128)(2,1)}, bf16[576,2048]{1,0:T(8,128)(2,1)S(1)}, u32[]{:S(2)}, u32[]{:S(2)}) collective-permute-start(bf16[576,2048]{1,0:T(8,128)(2,1)} %get-tuple-element.71.joined), channel_id=1, source_target_pairs={{0,64},{64,128},{128,192},{192,0},{1,65},{65,129},{129,193},{193,1... | collective-permute-start | bytes 7077896 | tf_op jit(solution)/shard_map/ppermute | solution.py:26
  171.8 53.7 %collective-permute-start.22 = (bf16[576,2048]{1,0:T(8,128)(2,1)}, bf16[576,2048]{1,0:T(8,128)(2,1)}, u32[]{:S(2)}, u32[]{:S(2)}) collective-permute-start(bf16[576,2048]{1,0:T(8,128)(2,1)} %get-tuple-element.86), channel_id=1, source_target_pairs={{0,192},{64,0},{128,64},{192,128},{1,193},{65,1},{129,65},{193,129... | collective-permute-start | bytes 7077896 | tf_op jit(solution)/shard_map/ppermute | solution.py:26
  179.8 12.6 %collective-permute-start.16 = (bf16[64,2176]{1,0:T(8,128)(2,1)}, bf16[64,2176]{1,0:T(8,128)(2,1)S(1)}, u32[]{:S(2)}, u32[]{:S(2)}) collective-permute-start(bf16[64,2176]{1,0:T(8,128)(2,1)} %get-tuple-element.80), channel_id=1, source_target_pairs={{0,14},{1,3},{2,0},{3,5},{4,2},{5,7},{6,4},{7,9},{8,6},{9,11},{10,... | collective-permute-start | bytes 835592 | tf_op jit(solution)/shard_map/ppermute | solution.py:339
  181.6 20.5 %collective-permute-start.17 = (bf16[64,2176]{1,0:T(8,128)(2,1)}, bf16[64,2176]{1,0:T(8,128)(2,1)S(1)}, u32[]{:S(2)}, u32[]{:S(2)}) collective-permute-start(bf16[64,2176]{1,0:T(8,128)(2,1)} %get-tuple-element.81), channel_id=1, source_target_pairs={{0,12},{1,5},{2,14},{3,7},{4,0},{5,9},{6,2},{7,11},{8,4},{9,13},{1... | collective-permute-start | bytes 835592 | tf_op jit(solution)/shard_map/ppermute | solution.py:339
  188.8 22.0 %collective-permute-start.18 = (bf16[64,2176]{1,0:T(8,128)(2,1)}, bf16[64,2176]{1,0:T(8,128)(2,1)S(1)}, u32[]{:S(2)}, u32[]{:S(2)}) collective-permute-start(bf16[64,2176]{1,0:T(8,128)(2,1)} %get-tuple-element.82), channel_id=1, source_target_pairs={{0,10},{1,7},{2,12},{3,9},{4,14},{5,11},{6,0},{7,13},{8,2},{9,15},... | collective-permute-start | bytes 835592 | tf_op jit(solution)/shard_map/ppermute | solution.py:339
  192.4 26.6 %collective-permute-start.14 = (bf16[32,2048]{1,0:T(8,128)(2,1)S(1)}, bf16[32,2048]{1,0:T(8,128)(2,1)S(1)}, u32[]{:S(2)}, u32[]{:S(2)}) collective-permute-start(bf16[32,2048]{1,0:T(8,128)(2,1)S(1)} %copy-done.11), channel_id=1, source_target_pairs={{0,8},{1,9},{2,10},{3,11},{4,12},{5,13},{6,14},{7,15},{8,0},{9,1},... | collective-permute-start | bytes 393224 | tf_op jit(solution)/shard_map/ppermute | solution.py:339
  202.1 18.6 %collective-permute-start.19 = (bf16[32,2176]{1,0:T(8,128)(2,1)S(1)}, bf16[32,2176]{1,0:T(8,128)(2,1)S(1)}, u32[]{:S(2)}, u32[]{:S(2)}) collective-permute-start(bf16[32,2176]{1,0:T(8,128)(2,1)S(1)} %copy-done.10), channel_id=1, source_target_pairs={{0,8},{1,9},{2,10},{3,11},{4,12},{5,13},{6,14},{7,15},{8,0},{9,1},... | collective-permute-start | bytes 417800 | tf_op jit(solution)/shard_map/ppermute | solution.py:339
  210.8 9.1 %collective-permute-start.15 = (bf16[32,2048]{1,0:T(8,128)(2,1)S(1)}, bf16[32,2048]{1,0:T(8,128)(2,1)S(1)}, u32[]{:S(2)}, u32[]{:S(2)}) collective-permute-start(bf16[32,2048]{1,0:T(8,128)(2,1)S(1)} %slice.82), channel_id=1, source_target_pairs={{0,1},{1,0},{2,3},{3,2},{4,5},{5,4},{6,7},{7,6},{8,9},{9,8},{10,11... | collective-permute-start | bytes 393224 | tf_op jit(solution)/shard_map/ppermute | solution.py:343
  (14 other events, 146.4 us)

commit v2 on v1

--- a/solution.py
+++ b/solution.py
@@ -11,7 +11,7 @@
 F32 = jnp.float32
 BF16 = jnp.bfloat16
 LANES = 128
-TILE = 512
+TILE = 1024
 PIECES = 5
 PLACES = ((0, 0), (0, 3), (1, 0), (1, 3), (2, 0), (2, 3), (3, 0), (4, 0))
 MIB = 56
@@ -32,9 +32,10 @@
     )
 
 
-def call(kernel, outs, in_specs, out_specs, scratch, flops, bytes_accessed, mib, name):
+def call(kernel, outs, in_specs, out_specs, scratch, flops, bytes_accessed, mib, name, grid=()):
     return pl.pallas_call(
         kernel,
+        grid=grid,
         out_shape=[jax.ShapeDtypeStruct(s, d) for s, d in outs],
         in_specs=in_specs,
         out_specs=out_specs,
@@ -45,6 +46,11 @@
         ),
         name=name,
     )
+
+
+def strips(shape):
+    lead = len(shape) - 1
+    return pl.BlockSpec(tuple(shape[:-1]) + (TILE,), lambda step: (0,) * lead + (step,))
 
 
 def split3(value):
@@ -137,7 +143,7 @@
     lax.fori_loop(0, width // TILE, columns, 0)
 
 
-def load(pieces, places, weights, sems):
+def load(pieces, places, weights, sems, skip=0):
     half = pieces[-1].shape[0] // 3
     copies = []
     for index, (number, first) in enumerate(places):
@@ -145,7 +151,7 @@
         for slot, (kind, weight) in enumerate(weights):
             copy = pltpu.make_async_copy(
                 pieces[number].at[pl.ds(first * half + kind * half, half), :],
-                weight.at[pl.ds(index * half, half), :],
+                weight.at[pl.ds((index + skip) * half, half), :],
                 sems.at[index * len(weights) + slot],
             )
             copy.start()
@@ -171,38 +177,61 @@
     return wide[:, :LANES] + wide[:, LANES:]
 
 
-def forward_kernel(arrived, *refs):
+def forward_kernel(arrived_hbm, *refs):
     pieces = refs[:PIECES]
-    gate_all, up_all, hid, result, gcot, ucot, score, grad_0, grad_1 = refs[PIECES : PIECES + 9]
-    hid_far, lefts, w_gate, w_up, w_down, sems = refs[PIECES + 9 :]
+    outs = refs[PIECES : PIECES + 6]
+    gcot, ucot, score = refs[PIECES + 6 : PIECES + 9]
+    held = refs[PIECES + 9 : PIECES + 15]
+    gate_all, up_all, hid, result, grad_0, grad_1 = held
+    arrived, hid_far, lefts, w_gate, w_up, w_down, sems, in_sems, out_sems = refs[PIECES + 15 :]
     dests, double, width = arrived.shape
     cap = double // 2
     count = dests * cap
     half = grad_0.shape[0] // 3
-    copies = load(pieces, PLACES, ((0, w_gate), (1, w_up), (2, w_down)), sems)
+    shards = len(PLACES) // 2
+    kinds = ((0, w_gate), (1, w_up), (2, w_down))
+    arrival = pltpu.make_async_copy(arrived_hbm, arrived, in_sems.at[0])
+    arrival.start()
+    copies = load(pieces, PLACES[-2:], kinds, sems.at[pl.ds(0, 6)])
+    arrival.wait()
+    wait_all(copies)
+    near = len(PLACES) - 2
+    copies = load(pieces, PLACES[:-2], kinds, sems.at[pl.ds(6, 3 * near)], 2)
     rows = arrived[:, :cap, :].reshape(count, width)
-    shards = len(PLACES) // 2
+    leaving = []
+
+    def leave(index):
+        copy = pltpu.make_async_copy(held[index], outs[index], out_sems.at[index])
+        copy.start()
+        leaving.append(copy)
+
     hidden = []
     for shard in range(shards):
-        wait_all(copies[2 * shard : 2 * shard + 2])
+        if shard:
+            wait_all(copies[2 * shard - 2 : 2 * shard])
         span = slice(2 * shard * half, 2 * (shard + 1) * half)
         gate_pre = dot(rows, w_gate[span, :], 1, 1)
         up_pre = dot(rows, w_up[span, :], 1, 1)
         value = (gate_pre * jax.nn.sigmoid(gate_pre) * up_pre).astype(BF16)
-        if shard < shards - 1:
-            gate_all[shard], up_all[shard], hid[shard] = gate_pre, up_pre, value
-            hidden.append(hid.at[shard])
-    hid_far[...] = value
-    hidden.append(hid_far)
-    hidden_cot = dot(arrived[:, cap:, :].reshape(count, width), w_down[span, :], 1, 1)
-    gate_cot, up_cot = hidden_parts(gate_pre, up_pre, hidden_cot)
-    gcot[...] = gate_cot.astype(BF16)
-    ucot[...] = up_cot.astype(BF16)
-    score[...] = fold(value.astype(F32) * hidden_cot)
-    lefts[0] = gate_cot.T.astype(BF16)
-    lefts[1] = up_cot.T.astype(BF16)
-    lefts[2] = value.astype(F32).T.astype(BF16)
-    write_grads(arrived, lefts, (grad_0, grad_1))
+        if shard:
+            gate_all[shard - 1], up_all[shard - 1], hid[shard - 1] = gate_pre, up_pre, value
+            hidden.append(hid.at[shard - 1])
+            continue
+        hid_far[...] = value
+        hidden.append(hid_far)
+        hidden_cot = dot(arrived[:, cap:, :].reshape(count, width), w_down[span, :], 1, 1)
+        gate_cot, up_cot = hidden_parts(gate_pre, up_pre, hidden_cot)
+        gcot[...] = gate_cot.astype(BF16)
+        ucot[...] = up_cot.astype(BF16)
+        score[...] = fold(value.astype(F32) * hidden_cot)
+        lefts[0] = gate_cot.T.astype(BF16)
+        lefts[1] = up_cot.T.astype(BF16)
+        lefts[2] = value.astype(F32).T.astype(BF16)
+        write_grads(arrived, lefts, (grad_0, grad_1))
+        leave(4)
+        leave(5)
+    for index in range(3):
+        leave(index)
 
     def columns(step, carry):
         span = pl.ds(pl.multiple_of(step * TILE, TILE), TILE)
@@ -214,6 +243,9 @@
         return carry
 
     lax.fori_loop(0, width // TILE, columns, 0)
+    leave(3)
+    for copy in leaving:
+        copy.wait()
 
 
 def write_grads(arrived, lefts, pieces):
@@ -353,13 +385,22 @@
     return blocks
 
 
-def ring_reduce(blocks):
+def add(left, right):
+    return (left.astype(F32) + right.astype(F32)).astype(BF16)
+
+
+def ring_reduce(blocks, after=None):
     rows = blocks[0].shape[0]
     far = len(blocks) - 1
-    arrived = [along(blocks[step], -step).astype(F32) for step in range(1, far + 1)]
-    both = sum(arrived[:-1])
+    hop = along(blocks[far], -1)
+    arrived = [along(blocks[step], -step) for step in range(1, far - 1)]
+    last = add(blocks[far - 1], jnp.pad(hop, ((0, rows), (0, 0))))
+    arrived.append(along(last, 1 - far))
+    if after is not None:
+        *arrived, _ = lax.optimization_barrier((*arrived, after))
+    both = sum(value.astype(F32) for value in arrived)
     other = swap(both[rows:].astype(BF16))
-    return blocks[0].astype(F32) + both[:rows] + arrived[-1] + other.astype(F32)
+    return blocks[0].astype(F32) + both[:rows] + other.astype(F32)
 
 
 def merge_kernel(first_0, relayed_0, second_0, first_1, relayed_1, second_1, joined_0, joined_1):
@@ -430,13 +471,14 @@
     (own,) = call(
         weights_kernel,
         [((2 * three, width), BF16)],
-        [VMEM] * 2,
-        [VMEM],
+        [strips(gate_up.shape), strips(down_weight.shape)],
+        [strips((2 * three, width))],
         [],
         0,
         0,
         MIB,
         "weights",
+        (width // TILE,),
     )(gate_up, down_weight)
     before = shift(own, "dp", 1)
     after = shift(own, "dp", -1)
@@ -454,7 +496,8 @@
         MIB,
         "select",
     )(z_index, *blocks)
-    before, after, _ = lax.optimization_barrier((before, after, send))
+    before, _ = lax.optimization_barrier((before, send))
+    after, _ = lax.optimization_barrier((after, send))
     far_0 = shift(before[:three], "dp", 1)
     far_1 = shift(after[three:], "dp", -1)
     far_0, far_1 = touch(far_0, far_1, "touch")
@@ -466,17 +509,18 @@
     hidden_type = ((count, units), BF16)
     piece_type = ((3 * half, width), BF16)
     weight = pltpu.VMEM((full, width), BF16)
-    gate_all, up_all, hid, result, gcot_f, ucot_f, score_f, far_g0, far_g1 = call(
+    held_types = [((shards, count, units), F32)] * 2 + [((shards, count, units), BF16), rows_type]
+    held_types = held_types + [piece_type] * 2
+    gate_all, up_all, hid, result, far_g0, far_g1, gcot_f, ucot_f, score_f = call(
         forward_kernel,
-        [((shards, count, units), F32)] * 2
-        + [((shards, count, units), BF16), rows_type, hidden_type, hidden_type]
-        + [((count, LANES), F32)]
-        + [piece_type] * 2,
-        [VMEM] + [ANY] * len(pieces),
-        [VMEM] * 9,
-        [pltpu.VMEM((count, units), BF16), pltpu.VMEM((3, units, count), BF16)]
+        held_types + [hidden_type, hidden_type, ((count, LANES), F32)],
+        [ANY] * (1 + len(pieces)),
+        [ANY] * 6 + [VMEM] * 3,
+        [pltpu.VMEM(s, d) for s, d in held_types]
+        + [pltpu.VMEM((dests, 2 * cap, width), BF16)]
+        + [pltpu.VMEM((count, units), BF16), pltpu.VMEM((3, units, count), BF16)]
         + [weight] * 3
-        + [pltpu.SemaphoreType.DMA((3 * n,))],
+        + [pltpu.SemaphoreType.DMA((k,)) for k in (3 * n, 1, 6)],
         1,
         0,
         MIB,
@@ -503,13 +547,14 @@
     joined_0, joined_1 = call(
         merge_kernel,
         [((2 * three, width), BF16)] * 2,
-        [VMEM] * 6,
-        [VMEM] * 2,
+        [strips((three, width))] * 6,
+        [strips((2 * three, width))] * 2,
         [],
         1,
         0,
         MIB,
         "merge",
+        (width // TILE,),
     )(after_g0, relay_0, after_g1, before_g1, relay_1, before_g0)
     got_before = shift(joined_0, "dp", 1)
     got_after = shift(joined_1, "dp", -1)
@@ -517,13 +562,14 @@
     gate_up_grad, down_grad = call(
         final_kernel,
         [(gate_up.shape, F32), (down_weight.shape, F32)],
-        [VMEM] * 4,
-        [VMEM] * 2,
+        [strips((three, width))] * 2 + [strips((2 * three, width))] * 2,
+        [strips(gate_up.shape), strips(down_weight.shape)],
         [],
         0,
         0,
         MIB,
         "final",
+        (width // TILE,),
     )(own_0, own_1, got_before, got_after)
 
     back = lax.all_to_all(result, ("x", "c"), 0, 0, tiled=True)
@@ -551,7 +597,7 @@
         MIB,
         "combine_cot",
     )(back_cot, pick, slot_gate, slot_place)
-    summed = ring_reduce(list(parts))
+    summed = ring_reduce(list(parts), down_grad)
     token_grad = summed[:, :width].astype(BF16)
     tail = summed[:, width:]
     gate_grad = tail[:, :top] + tail[:, top : 2 * top] + tail[:, 2 * top : 3 * top]

time: 235 us -> 223 us (0.949)
  Pallas kernels: 68.1 us -> 59.5 us
  starting transfers between devices: 61.9 us -> 56.3 us
  other arithmetic: 2.03 us -> 6.07 us
    ppermute x12, waiting for transfers between devices: 42.9 us -> 34.2 us  [along(): return lax.ppermute(value, ('z', 'c'), pairs)]
    pallas_call x4, Pallas kernels: 34.4 us -> 28.5 us  [the longest x1 12.9 us: body(): call(forward_kernel, held_types + [hidden_type, hidden_type, ((count, LAN...]
    ppermute x8, waiting for transfers between devices: 46.1 us -> 50.7 us  [shift(): lax.ppermute(value, axis, [(i, (i + step) % size) for i in range(size)])]
    ppermute x3, starting transfers between devices: 11.4 us -> 7.24 us  [swap(): return lax.ppermute(value, 'c', [(0, 1), (1, 0)])]
    ppermute x12, starting transfers between devices: 22.8 us -> 19.6 us  [along(): return lax.ppermute(value, ('z', 'c'), pairs)]
    all_to_all x1, waiting for transfers between devices: 1.01 us -> 4.13 us  [body(): back_cot = lax.all_to_all(result_cot, ('x', 'c'), 0, 0, tiled=True)]
    unnamed x25 -> x27, local copies, waits for them, and re-layouts: 5.64 us -> 4.24 us
  transfers between devices with their start and end apart: 26 -> 26, of which waited for: 18 -> 14; matrix products, arithmetic and copies ran while one was open for 2% -> 4% of each run, Pallas kernels for 19% -> 20%
where the time goes in v2:
time: 223 us
  waiting for transfers between devices  91.7 us (41%)
  Pallas kernels  59.5 us (27%)
  starting transfers between devices  56.3 us (25%)
  local copies, waits for them, and re-layouts  8.39 us (4%)
  other arithmetic  6.07 us (3%)
    ppermute x8, waiting for transfers between devices, shift(): lax.ppermute(value, axis, [(i, (i + step) % size) for i in range(size)])  50.7 us
    ppermute x12, waiting for transfers between devices, along(): return lax.ppermute(value, ('z', 'c'), pairs)  34.2 us
    ppermute x12, starting transfers between devices, along(): return lax.ppermute(value, ('z', 'c'), pairs)  19.6 us
    pallas_call x1, Pallas kernels, body(): call(backward_kernel, [((dests, cap, wide), BF16)] + [piece_type] * (n -...  16.8 us
    pallas_call x1, Pallas kernels, body(): call(forward_kernel, held_types + [hidden_type, hidden_type, ((count, LAN...  12.9 us
    ppermute x8, starting transfers between devices, shift(): lax.ppermute(value, axis, [(i, (i + step) % size) for i in range(size)])  11.2 us
    all_to_all x1, starting transfers between devices, body(): arrived = lax.all_to_all(send, ('x', 'c'), 0, 0, tiled=True)  8.64 us
    ppermute x3, starting transfers between devices, swap(): return lax.ppermute(value, 'c', [(0, 1), (1, 0)])  7.24 us
  transfers between devices with their start and end apart: 26, of which 14 were waited for; matrix products, arithmetic and copies ran while one was open for 4% of the time, Pallas kernels for 20%

profile of v2, /device:TPU:1, one launch (start us, length us, event | category | flops | bytes accessed | tf_op | source)
XLA Modules:
  0.0 222.8 jit_solution(14633852845589861999)
XLA Ops:
  8.2 3.9 %collective-permute-start.1 = (bf16[64,4224]{1,0:T(8,128)(2,1)S(1)}, bf16[64,4224]{1,0:T(8,128)(2,1)S(1)}, u32[]{:S(2)}, u32[]{:S(2)}) collective-permute-start(bf16[64,4224]{1,0:T(8,128)(2,1)S(1)} %pad_maximum_fusion), channel_id=1, source_target_pairs={{0,2},{1,15},{2,4},{3,1},{4,6},{5,3},{6,8},{7,5},{8,10},{9,7},{10,... | collective-permute-start | bytes 1622024 | tf_op jit(solution)/shard_map/ppermute | solution.py:371
  12.1 5.8 %weights.1.refs_0_ = bf16[576,2048]{1,0:T(8,128)(2,1)} custom-call(bf16[1,192,2,2048]{3,2,1,0:T(2,128)(2,1)} %gate_up, bf16[1,192,2048]{2,1,0:T(8,128)(2,1)} %down), custom_call_target="tpu_custom_call" | custom-call | flops 10000000000 | tf_op jit(solution)/shard_map/weights/pallas_call | solution.py:471
  21.5 7.8 %collective-permute-done.2.refs_2_ = bf16[64,4224]{1,0:T(8,128)(2,1)S(1)} collective-permute-done((bf16[64,4224]{1,0:T(8,128)(2,1)S(1)}, bf16[64,4224]{1,0:T(8,128)(2,1)S(1)}, u32[]{:S(2)}, u32[]{:S(2)}) %collective-permute-start.2) | collective-permute-done | bytes 540704 | tf_op jit(solution)/shard_map/ppermute | solution.py:371
  31.3 6.6 %collective-permute-done.3.refs_3_ = bf16[64,4224]{1,0:T(8,128)(2,1)S(1)} collective-permute-done((bf16[64,4224]{1,0:T(8,128)(2,1)S(1)}, bf16[64,4224]{1,0:T(8,128)(2,1)S(1)}, u32[]{:S(2)}, u32[]{:S(2)}) %collective-permute-start.3) | collective-permute-done | bytes 540704 | tf_op jit(solution)/shard_map/ppermute | solution.py:371
  41.2 3.4 %collective-permute-done.4.refs_4_ = bf16[32,4224]{1,0:T(8,128)(2,1)S(1)} collective-permute-done((bf16[32,4224]{1,0:T(8,128)(2,1)S(1)}, bf16[32,4224]{1,0:T(8,128)(2,1)S(1)}, u32[]{:S(2)}, u32[]{:S(2)}) %collective-permute-start.4) | collective-permute-done | bytes 270368 | tf_op jit(solution)/shard_map/ppermute | solution.py:371
  45.4 4.9 %select.3 = (bf16[8,96,2048]{2,1,0:T(8,128)(2,1)}, bf16[384,256]{1,0:T(8,128)(2,1)}, f32[384,128]{1,0:T(8,128)}, f32[384,128]{1,0:T(8,128)}) custom-call(s32[1]{0:T(128)} %bitcast.z_index, bf16[32,4224]{1,0:T(8,128)(2,1)} %pack.1.refs_0_, bf16[64,4224]{1,0:T(8,128)(2,1)} %copy-done.4, bf16[64,4224]{1,0:T(8,128)(2,1)} %copy-done.5, ...), custom_call_target="tpu_custom_call" | custom-call | tf_op jit(solution)/shard_map/select/pallas_call | solution.py:488
  50.3 8.6 %all-to-all-start = ((bf16[8,96,2048]{2,1,0:T(8,128)(2,1)}), bf16[8,96,2048]{2,1,0:T(8,128)(2,1)S(1)}, u32[]{:S(2)}, u32[]{:S(2)}) async-start(bf16[8,96,2048]{2,1,0:T(8,128)(2,1)} %get-tuple-element.52), calls=%async_computation | async-start | bytes 6291456 | tf_op jit(solution)/shard_map/all_to_all | solution.py:506
  58.9 10.2 %collective-permute-done.6.refs_2_ = bf16[576,2048]{1,0:T(8,128)(2,1)} collective-permute-done((bf16[576,2048]{1,0:T(8,128)(2,1)}, bf16[576,2048]{1,0:T(8,128)(2,1)}, u32[]{:S(2)}, u32[]{:S(2)}) %collective-permute-start.6) | collective-permute-done | bytes 2359328 | tf_op jit(solution)/shard_map/ppermute | solution.py:26
  70.5 3.4 %collective-permute-start.8 = (bf16[288,2048]{1,0:T(8,128)(2,1)S(1)}, bf16[288,2048]{1,0:T(8,128)(2,1)}, u32[]{:S(2)}, u32[]{:S(2)}) collective-permute-start(bf16[288,2048]{1,0:T(8,128)(2,1)S(1)} %slice.42), channel_id=1, source_target_pairs={{0,192},{64,0},{128,64},{192,128},{1,193},{65,1},{129,65},{193,129... | collective-permute-start | bytes 3538952 | tf_op jit(solution)/shard_map/ppermute | solution.py:26
  75.6 22.2 %collective-permute-done.8.right = bf16[288,2048]{1,0:T(8,128)(2,1)} collective-permute-done((bf16[288,2048]{1,0:T(8,128)(2,1)S(1)}, bf16[288,2048]{1,0:T(8,128)(2,1)}, u32[]{:S(2)}, u32[]{:S(2)}) %collective-permute-start.8) | collective-permute-done | bytes 1179680 | tf_op jit(solution)/shard_map/ppermute | solution.py:26
  97.8 5.2 %collective-permute-done.7.left = bf16[288,2048]{1,0:T(8,128)(2,1)} collective-permute-done((bf16[288,2048]{1,0:T(8,128)(2,1)S(1)}, bf16[288,2048]{1,0:T(8,128)(2,1)}, u32[]{:S(2)}, u32[]{:S(2)}) %collective-permute-start.7) | collective-permute-done | bytes 1179680 | tf_op jit(solution)/shard_map/ppermute | solution.py:26
  104.6 12.9 %forward.1 = (f32[3,384,192]{2,1,0:T(8,128)}, f32[3,384,192]{2,1,0:T(8,128)}, bf16[3,384,192]{2,1,0:T(8,128)(2,1)}, bf16[8,48,2048]{2,1,0:T(8,128)(2,1)}, bf16[2...) custom-call(bf16[8,96,2048]{2,1,0:T(8,128)(2,1)} %copy-done, ...), custom_call_target="tpu_custom_call" | custom-call | flops 1000000000 | tf_op jit(solution)/shard_map/forward/pallas_call | solution.py:514
  117.6 4.5 %all-to-all-start.1 = ((bf16[8,48,2048]{2,1,0:T(8,128)(2,1)}), bf16[8,48,2048]{2,1,0:T(8,128)(2,1)S(1)}, u32[]{:S(2)}, u32[]{:S(2)}) async-start(bf16[8,48,2048]{2,1,0:T(8,128)(2,1)} %get-tuple-element.59), calls=%async_computation.1 | async-start | bytes 3145728 | tf_op jit(solution)/shard_map/all_to_all | solution.py:575
  124.8 16.8 %backward.1 = (bf16[8,48,2176]{2,1,0:T(8,128)(2,1)}, bf16[288,2048]{1,0:T(8,128)(2,1)}, bf16[288,2048]{1,0:T(8,128)(2,1)}, bf16[288,2048]{1,0:T(8,128)(2,1)}, bf...) custom-call(bf16[8,96,2048]{2,1,0:T(8,128)(2,1)} %copy-done, ...), custom_call_target="tpu_custom_call" | custom-call | flops 1000000000 | tf_op jit(solution)/shard_map/backward/pallas_call | solution.py:529
  144.0 5.1 %all-to-all-start.2 = ((bf16[8,48,2176]{2,1,0:T(8,128)(2,1)}), bf16[8,48,2176]{2,1,0:T(8,128)(2,1)}, u32[]{:S(2)}, u32[]{:S(2)}) async-start(bf16[8,48,2176]{2,1,0:T(8,128)(2,1)} %get-tuple-element.80), calls=%async_computation.2 | async-start | bytes 3342336 | tf_op jit(solution)/shard_map/all_to_all | solution.py:588
  151.2 4.7 %merge.1 = (bf16[576,2048]{1,0:T(8,128)(2,1)}, bf16[576,2048]{1,0:T(8,128)(2,1)}) custom-call(bf16[288,2048]{1,0:T(8,128)(2,1)} %get-tuple-element.68.first_0, bf16[288,2048]{1,0:T(8,128)(2,1)} %collective-permute-done.9.relayed_0, bf16[288,2048]{1,0:T(8,128)(2,1)} %get-tuple-element.70.second_0, bf16[288,2048]{1,0:T(8,128)(2,1)} %get-tuple-element.71.first_1, ...), custom_call_target="tpu_custom_call" | custom-call | flops 80000000000 | tf_op jit(solution)/shard_map/merge/pallas_call | solution.py:547
  158.1 3.5 %combine.1 = (bf16[32,2048]{1,0:T(8,128)(2,1)}, bf16[64,2048]{1,0:T(8,128)(2,1)}, bf16[64,2048]{1,0:T(8,128)(2,1)}, bf16[64,2048]{1,0:T(8,128)(2,1)}, bf16[32,2048]{1,0:T(8,128)(2,1)}) custom-call(bf16[8,48,2048]{2,1,0:T(8,128)(2,1)} %copy-done.2, bf16[384,256]{1,0:T(8,128)(2,1)} %get-tuple-element.60.pick, f32[384,128]{1,0:T(8,128)} %get-tuple-element.61.slot_gate, ...), custom_call_target="tpu_custom_call" | custom-call | tf_op jit(solution)/shard_map/combine/pallas_call | solution.py:576
  161.7 5.1 %collective-permute-start.12 = (bf16[64,2048]{1,0:T(8,128)(2,1)}, bf16[64,2048]{1,0:T(8,128)(2,1)S(1)}, u32[]{:S(2)}, u32[]{:S(2)}) collective-permute-start(bf16[64,2048]{1,0:T(8,128)(2,1)} %get-tuple-element.77), channel_id=1, source_target_pairs={{0,12},{1,5},{2,14},{3,7},{4,0},{5,9},{6,2},{7,11},{8,4},{9,13},{1... | collective-permute-start | bytes 786440 | tf_op jit(solution)/shard_map/ppermute | solution.py:371
  166.8 4.1 %all-to-all-done.2.back = bf16[8,48,2176]{2,1,0:T(8,128)(2,1)} async-done(((bf16[8,48,2176]{2,1,0:T(8,128)(2,1)}), bf16[8,48,2176]{2,1,0:T(8,128)(2,1)}, u32[]{:S(2)}, u32[]{:S(2)}) %all-to-all-start.2) | async-done | bytes 1671200 | tf_op jit(solution)/shard_map/all_to_all | solution.py:588
  170.9 4.0 %combine_cot.1 = (bf16[32,2176]{1,0:T(8,128)(2,1)}, bf16[64,2176]{1,0:T(8,128)(2,1)}, bf16[64,2176]{1,0:T(8,128)(2,1)}, bf16[64,2176]{1,0:T(8,128)(2,1)}, bf16[32,2176]{1,0:T(8,128)(2,1)}) custom-call(bf16[8,48,2176]{2,1,0:T(8,128)(2,1)} %all-to-all-done.2.back, bf16[384,256]{1,0:T(8,128)(2,1)} %get-tuple-element.60.pick, ...), custom_call_target="tpu_custom_call" | custom-call | tf_op jit(solution)/shard_map/combine_cot/pallas_call | solution.py:589
  175.0 8.8 %collective-permute-done.18 = bf16[32,2176]{1,0:T(8,128)(2,1)S(1)} collective-permute-done((bf16[32,2176]{1,0:T(8,128)(2,1)}, bf16[32,2176]{1,0:T(8,128)(2,1)S(1)}, u32[]{:S(2)}, u32[]{:S(2)}) %collective-permute-start.18) | collective-permute-done | bytes 139296 | tf_op jit(solution)/shard_map/ppermute | solution.py:371
  188.1 7.7 %collective-permute-done.14 = bf16[64,2048]{1,0:T(8,128)(2,1)S(1)} collective-permute-done((bf16[64,2048]{1,0:T(8,128)(2,1)S(1)}, bf16[64,2048]{1,0:T(8,128)(2,1)S(1)}, u32[]{:S(2)}, u32[]{:S(2)}) %collective-permute-start.14) | collective-permute-done | bytes 262176 | tf_op jit(solution)/shard_map/ppermute | solution.py:371
  198.4 9.9 %collective-permute-done.21.right = bf16[576,2048]{1,0:T(8,128)(2,1)S(1)} collective-permute-done((bf16[576,2048]{1,0:T(8,128)(2,1)}, bf16[576,2048]{1,0:T(8,128)(2,1)S(1)}, u32[]{:S(2)}, u32[]{:S(2)}) %collective-permute-start.21) | collective-permute-done | bytes 2359328 | tf_op jit(solution)/shard_map/ppermute | solution.py:26
  211.0 5.0 %final.1 = (f32[1,192,2,2048]{3,2,1,0:T(2,128)}, f32[1,192,2048]{2,1,0:T(8,128)}) custom-call(bf16[288,2048]{1,0:T(8,128)(2,1)} %get-tuple-element.87.own_0, bf16[288,2048]{1,0:T(8,128)(2,1)} %get-tuple-element.88.own_1, bf16[576,2048]{1,0:T(8,128)(2,1)} %get-tuple-element.90.before, bf16[576,2048]{1,0:T(8,128)(2,1)} %get-tuple-element.91.after), custom_call_target="tpu_custom_call" | custom-call | tf_op jit(solution)/shard_map/final/pallas_call | solution.py:562
  (80 shorter events, 47.9 us)
Async XLA Ops:
  8.2 12.4 %collective-permute-start.1 = (bf16[64,4224]{1,0:T(8,128)(2,1)S(1)}, bf16[64,4224]{1,0:T(8,128)(2,1)S(1)}, u32[]{:S(2)}, u32[]{:S(2)}) collective-permute-start(bf16[64,4224]{1,0:T(8,128)(2,1)S(1)} %pad_maximum_fusion), channel_id=1, source_target_pairs={{0,2},{1,15},{2,4},{3,1},{4,6},{5,3},{6,8},{7,5},{8,10},{9,7},{10,... | collective-permute-start | bytes 1622024 | tf_op jit(solution)/shard_map/ppermute | solution.py:371
  17.8 51.3 %collective-permute-start.6 = (bf16[576,2048]{1,0:T(8,128)(2,1)}, bf16[576,2048]{1,0:T(8,128)(2,1)}, u32[]{:S(2)}, u32[]{:S(2)}) collective-permute-start(bf16[576,2048]{1,0:T(8,128)(2,1)} %weights.1.refs_0_), channel_id=1, source_target_pairs={{0,192},{64,0},{128,64},{192,128},{1,193},{65,1},{129,65},{193,129... | collective-permute-start | bytes 7077896 | tf_op jit(solution)/shard_map/ppermute | solution.py:26
  20.6 53.3 %collective-permute-start.5 = (bf16[576,2048]{1,0:T(8,128)(2,1)}, bf16[576,2048]{1,0:T(8,128)(2,1)}, u32[]{:S(2)}, u32[]{:S(2)}) collective-permute-start(bf16[576,2048]{1,0:T(8,128)(2,1)} %weights.1.refs_0_), channel_id=1, source_target_pairs={{0,64},{64,128},{128,192},{192,0},{1,65},{65,129},{129,193},{193,1... | collective-permute-start | bytes 7077896 | tf_op jit(solution)/shard_map/ppermute | solution.py:26
  20.6 8.7 %collective-permute-start.2 = (bf16[64,4224]{1,0:T(8,128)(2,1)S(1)}, bf16[64,4224]{1,0:T(8,128)(2,1)S(1)}, u32[]{:S(2)}, u32[]{:S(2)}) collective-permute-start(bf16[64,4224]{1,0:T(8,128)(2,1)S(1)} %collective-permute-done.1.refs_1_), channel_id=1, source_target_pairs={{0,2},{1,15},{2,4},{3,1},{4,6},{5,3},{6,8},{7,5},{8,10},{9,7},{10,... | collective-permute-start | bytes 1622024 | tf_op jit(solution)/shard_map/ppermute | solution.py:371
  29.3 8.6 %collective-permute-start.3 = (bf16[64,4224]{1,0:T(8,128)(2,1)S(1)}, bf16[64,4224]{1,0:T(8,128)(2,1)S(1)}, u32[]{:S(2)}, u32[]{:S(2)}) collective-permute-start(bf16[64,4224]{1,0:T(8,128)(2,1)S(1)} %collective-permute-done.2.refs_2_), channel_id=1, source_target_pairs={{0,2},{1,15},{2,4},{3,1},{4,6},{5,3},{6,8},{7,5},{8,10},{9,7},{10,... | collective-permute-start | bytes 1622024 | tf_op jit(solution)/shard_map/ppermute | solution.py:371
  37.9 6.7 %collective-permute-start.4 = (bf16[32,4224]{1,0:T(8,128)(2,1)S(1)}, bf16[32,4224]{1,0:T(8,128)(2,1)S(1)}, u32[]{:S(2)}, u32[]{:S(2)}) collective-permute-start(bf16[32,4224]{1,0:T(8,128)(2,1)S(1)} %slice.51), channel_id=1, source_target_pairs={{0,2},{1,15},{2,4},{3,1},{4,6},{5,3},{6,8},{7,5},{8,10},{9,7},{10,... | collective-permute-start | bytes 811016 | tf_op jit(solution)/shard_map/ppermute | solution.py:371
  50.3 52.6 %all-to-all-start = ((bf16[8,96,2048]{2,1,0:T(8,128)(2,1)}), bf16[8,96,2048]{2,1,0:T(8,128)(2,1)S(1)}, u32[]{:S(2)}, u32[]{:S(2)}) async-start(bf16[8,96,2048]{2,1,0:T(8,128)(2,1)} %get-tuple-element.52), calls=%async_computation | async-start | bytes 6291456 | tf_op jit(solution)/shard_map/all_to_all | solution.py:506
  70.5 27.2 %collective-permute-start.8 = (bf16[288,2048]{1,0:T(8,128)(2,1)S(1)}, bf16[288,2048]{1,0:T(8,128)(2,1)}, u32[]{:S(2)}, u32[]{:S(2)}) collective-permute-start(bf16[288,2048]{1,0:T(8,128)(2,1)S(1)} %slice.42), channel_id=1, source_target_pairs={{0,192},{64,0},{128,64},{192,128},{1,193},{65,1},{129,65},{193,129... | collective-permute-start | bytes 3538952 | tf_op jit(solution)/shard_map/ppermute | solution.py:26
  75.3 27.6 %collective-permute-start.7 = (bf16[288,2048]{1,0:T(8,128)(2,1)S(1)}, bf16[288,2048]{1,0:T(8,128)(2,1)}, u32[]{:S(2)}, u32[]{:S(2)}) collective-permute-start(bf16[288,2048]{1,0:T(8,128)(2,1)S(1)} %slice.41), channel_id=1, source_target_pairs={{0,64},{64,128},{128,192},{192,0},{1,65},{65,129},{129,193},{193,1... | collective-permute-start | bytes 3538952 | tf_op jit(solution)/shard_map/ppermute | solution.py:26
  117.6 25.3 %all-to-all-start.1 = ((bf16[8,48,2048]{2,1,0:T(8,128)(2,1)}), bf16[8,48,2048]{2,1,0:T(8,128)(2,1)S(1)}, u32[]{:S(2)}, u32[]{:S(2)}) async-start(bf16[8,48,2048]{2,1,0:T(8,128)(2,1)} %get-tuple-element.59), calls=%async_computation.1 | async-start | bytes 3145728 | tf_op jit(solution)/shard_map/all_to_all | solution.py:575
  122.1 29.1 %collective-permute-start.9 = (bf16[288,2048]{1,0:T(8,128)(2,1)}, bf16[288,2048]{1,0:T(8,128)(2,1)}, u32[]{:S(2)}, u32[]{:S(2)}) collective-permute-start(bf16[288,2048]{1,0:T(8,128)(2,1)} %get-tuple-element.69), channel_id=1, source_target_pairs={{0,64},{64,128},{128,192},{192,0},{1,65},{65,129},{129,193},{193,1... | collective-permute-start | bytes 3538952 | tf_op jit(solution)/shard_map/ppermute | solution.py:26
  122.1 29.1 %collective-permute-start.10 = (bf16[288,2048]{1,0:T(8,128)(2,1)S(1)}, bf16[288,2048]{1,0:T(8,128)(2,1)}, u32[]{:S(2)}, u32[]{:S(2)}) collective-permute-start(bf16[288,2048]{1,0:T(8,128)(2,1)S(1)} %copy-done.12), channel_id=1, source_target_pairs={{0,192},{64,0},{128,64},{192,128},{1,193},{65,1},{129,65},{193,129... | collective-permute-start | bytes 3538952 | tf_op jit(solution)/shard_map/ppermute | solution.py:26
  144.0 27.0 %all-to-all-start.2 = ((bf16[8,48,2176]{2,1,0:T(8,128)(2,1)}), bf16[8,48,2176]{2,1,0:T(8,128)(2,1)}, u32[]{:S(2)}, u32[]{:S(2)}) async-start(bf16[8,48,2176]{2,1,0:T(8,128)(2,1)} %get-tuple-element.80), calls=%async_computation.2 | async-start | bytes 3342336 | tf_op jit(solution)/shard_map/all_to_all | solution.py:588
  156.0 52.3 %collective-permute-start.21 = (bf16[576,2048]{1,0:T(8,128)(2,1)}, bf16[576,2048]{1,0:T(8,128)(2,1)S(1)}, u32[]{:S(2)}, u32[]{:S(2)}) collective-permute-start(bf16[576,2048]{1,0:T(8,128)(2,1)} %get-tuple-element.89), channel_id=1, source_target_pairs={{0,192},{64,0},{128,64},{192,128},{1,193},{65,1},{129,65},{193,129... | collective-permute-start | bytes 7077896 | tf_op jit(solution)/shard_map/ppermute | solution.py:26
  158.1 52.9 %collective-permute-start.20 = (bf16[576,2048]{1,0:T(8,128)(2,1)}, bf16[576,2048]{1,0:T(8,128)(2,1)}, u32[]{:S(2)}, u32[]{:S(2)}) collective-permute-start(bf16[576,2048]{1,0:T(8,128)(2,1)} %get-tuple-element.74.joined), channel_id=1, source_target_pairs={{0,64},{64,128},{128,192},{192,0},{1,65},{65,129},{129,193},{193,1... | collective-permute-start | bytes 7077896 | tf_op jit(solution)/shard_map/ppermute | solution.py:26
  161.6 13.3 %collective-permute-start.13 = (bf16[32,2048]{1,0:T(8,128)(2,1)}, bf16[32,2048]{1,0:T(8,128)(2,1)S(1)}, u32[]{:S(2)}, u32[]{:S(2)}) collective-permute-start(bf16[32,2048]{1,0:T(8,128)(2,1)} %get-tuple-element.79), channel_id=1, source_target_pairs={{0,14},{1,3},{2,0},{3,5},{4,2},{5,7},{6,4},{7,9},{8,6},{9,11},{10,... | collective-permute-start | bytes 393224 | tf_op jit(solution)/shard_map/ppermute | solution.py:371
  161.6 23.1 %collective-permute-start.11 = (bf16[64,2048]{1,0:T(8,128)(2,1)}, bf16[64,2048]{1,0:T(8,128)(2,1)S(1)}, u32[]{:S(2)}, u32[]{:S(2)}) collective-permute-start(bf16[64,2048]{1,0:T(8,128)(2,1)} %get-tuple-element.76), channel_id=1, source_target_pairs={{0,14},{1,3},{2,0},{3,5},{4,2},{5,7},{6,4},{7,9},{8,6},{9,11},{10,... | collective-permute-start | bytes 786440 | tf_op jit(solution)/shard_map/ppermute | solution.py:371
  161.7 24.9 %collective-permute-start.12 = (bf16[64,2048]{1,0:T(8,128)(2,1)}, bf16[64,2048]{1,0:T(8,128)(2,1)S(1)}, u32[]{:S(2)}, u32[]{:S(2)}) collective-permute-start(bf16[64,2048]{1,0:T(8,128)(2,1)} %get-tuple-element.77), channel_id=1, source_target_pairs={{0,12},{1,5},{2,14},{3,7},{4,0},{5,9},{6,2},{7,11},{8,4},{9,13},{1... | collective-permute-start | bytes 786440 | tf_op jit(solution)/shard_map/ppermute | solution.py:371
  174.9 8.8 %collective-permute-start.18 = (bf16[32,2176]{1,0:T(8,128)(2,1)}, bf16[32,2176]{1,0:T(8,128)(2,1)S(1)}, u32[]{:S(2)}, u32[]{:S(2)}) collective-permute-start(bf16[32,2176]{1,0:T(8,128)(2,1)} %get-tuple-element.86), channel_id=1, source_target_pairs={{0,14},{1,3},{2,0},{3,5},{4,2},{5,7},{6,4},{7,9},{8,6},{9,11},{10,... | collective-permute-start | bytes 417800 | tf_op jit(solution)/shard_map/ppermute | solution.py:371
  183.7 12.0 %collective-permute-start.14 = (bf16[64,2048]{1,0:T(8,128)(2,1)S(1)}, bf16[64,2048]{1,0:T(8,128)(2,1)S(1)}, u32[]{:S(2)}, u32[]{:S(2)}) collective-permute-start(bf16[64,2048]{1,0:T(8,128)(2,1)S(1)} %add_convert_fusion.1), channel_id=1, source_target_pairs={{0,10},{1,7},{2,12},{3,9},{4,14},{5,11},{6,0},{7,13},{8,2},{9,15},... | collective-permute-start | bytes 786440 | tf_op jit(solution)/shard_map/ppermute | solution.py:371
  184.8 31.3 %collective-permute-start.16 = (bf16[64,2176]{1,0:T(8,128)(2,1)}, bf16[64,2176]{1,0:T(8,128)(2,1)S(1)}, u32[]{:S(2)}, u32[]{:S(2)}) collective-permute-start(bf16[64,2176]{1,0:T(8,128)(2,1)} %get-tuple-element.83), channel_id=1, source_target_pairs={{0,14},{1,3},{2,0},{3,5},{4,2},{5,7},{6,4},{7,9},{8,6},{9,11},{10,... | collective-permute-start | bytes 835592 | tf_op jit(solution)/shard_map/ppermute | solution.py:371
  186.7 29.4 %collective-permute-start.17 = (bf16[64,2176]{1,0:T(8,128)(2,1)}, bf16[64,2176]{1,0:T(8,128)(2,1)}, u32[]{:S(2)}, u32[]{:S(2)}) collective-permute-start(bf16[64,2176]{1,0:T(8,128)(2,1)} %get-tuple-element.84), channel_id=1, source_target_pairs={{0,12},{1,5},{2,14},{3,7},{4,0},{5,9},{6,2},{7,11},{8,4},{9,13},{1... | collective-permute-start | bytes 835592 | tf_op jit(solution)/shard_map/ppermute | solution.py:371
  195.8 20.3 %collective-permute-start.19 = (bf16[64,2176]{1,0:T(8,128)(2,1)S(1)}, bf16[64,2176]{1,0:T(8,128)(2,1)}, u32[]{:S(2)}, u32[]{:S(2)}) collective-permute-start(bf16[64,2176]{1,0:T(8,128)(2,1)S(1)} %add_convert_fusion), channel_id=1, source_target_pairs={{0,10},{1,7},{2,12},{3,9},{4,14},{5,11},{6,0},{7,13},{8,2},{9,15},... | collective-permute-start | bytes 835592 | tf_op jit(solution)/shard_map/ppermute | solution.py:371
  208.3 11.4 %collective-permute-start.15 = (bf16[32,2048]{1,0:T(8,128)(2,1)}, bf16[32,2048]{1,0:T(8,128)(2,1)}, u32[]{:S(2)}, u32[]{:S(2)}) collective-permute-start(bf16[32,2048]{1,0:T(8,128)(2,1)} %slice.78), channel_id=1, source_target_pairs={{0,1},{1,0},{2,3},{3,2},{4,5},{5,4},{6,7},{7,6},{8,9},{9,8},{10,11... | collective-permute-start | bytes 393224 | tf_op jit(solution)/shard_map/ppermute | solution.py:375
  (15 other events, 108.1 us)
